TPU v7x, 512 devices: a whole 4x4x16 slice. The times are simulated.
512 devices in a mesh: lat: 128 (over z, x_lo, y), lon: 4 (over x_hi, core).
Axes of the slice: x: 4 (x_hi: 2, x_lo: 2; x = x_hi * 2 + x_lo), y: 4, z: 16, core: 2. Of those that a mesh axis runs over, the one named last changes fastest.
Arguments:
- tokens: bfloat16 [128, 512, 640], P('lat', 'lon'), may hold values from -6 to 6
- cotangent: bfloat16 [128, 512, 640], P('lat', 'lon'), may hold values from -6 to 6
- raw_obs: bfloat16 [262144, 64], P(('lat', 'lon')), may hold values from -6 to 6
- obs_band: int32 [262144, 1], P(('lat', 'lon')), may hold values from 0 to 127; in each aligned block of 512 rows (0 to 511, 512 to 1023, ...) at most 8 rows name the same one
- obs_slot: int32 [262144], P(('lat', 'lon')), may hold values from 0 to 127
- obs_inst: int32 [262144], P(('lat', 'lon')), may hold values from 0 to 31
- obs_count: int32 [512], P(('lat', 'lon')), may hold values from 256 to 512, as said below
- w_key_obs: bfloat16 [64, 640], replicated, may hold values from -0.75 to 0.75
- w_val_obs: bfloat16 [64, 640], replicated, may hold values from -0.75 to 0.75
- inst_table: bfloat16 [32, 640], replicated, may hold values from -6 to 6
- null_key: bfloat16 [640], replicated, may hold values from -6 to 6
- null_val: bfloat16 [640], replicated, may hold values from -6 to 6
- w_query: bfloat16 [640, 640], replicated, may hold values from -0.25 to 0.25
- norm_gain: float32 [640], replicated, may hold values from 0.1 to 1.9
- zonal_query: bfloat16 [640, 640], replicated, may hold values from -0.25 to 0.25
- zonal_key: bfloat16 [640, 640], replicated, may hold values from -0.25 to 0.25
- zonal_value: bfloat16 [640, 640], replicated, may hold values from -0.25 to 0.25
- zonal_out: bfloat16 [640, 640], replicated, may hold values from -0.25 to 0.25
Outputs:
- d_tokens: bfloat16 [128, 512, 640], P('lat', 'lon')
- key_grad: float32 [64, 640], replicated
- value_grad: float32 [64, 640], replicated
Inputs may be any that keep to these rules, and one draw needn't show every extreme that they name: `obs_band`: among the 512 rows of one ingest device, no latitude row is named more than 8 times. The live rows of an ingest device are its first obs_count rows.
All inputs are finite; a program needn't handle non-finite values.
Results may differ from a plain program's by a relative error of at most 0.015.
Values may be sent and summed in bfloat16 or wider, within the bound.
No kernel may reach another device: no remote copies, remote signals or barrier semaphores. Data moves between devices by JAX's collectives and lax.ppermute only.
A program may use at most 128 MiB of HBM per device.

v0:
```python
import math

import jax
import jax.numpy as jnp
from jax import lax
from jax.sharding import PartitionSpec as P

HEAD_DIM = 64


logit_cap = 6.0
norm_eps = 1e-06


def capped(raw_score):
    return logit_cap * jnp.tanh(raw_score / logit_cap)


def cap_slope(raw_score):
    inner_tanh = jnp.tanh(raw_score / logit_cap)
    return 1.0 - inner_tanh * inner_tanh


def silu_slope(value):
    sigma = jax.nn.sigmoid(value)
    return sigma * (1.0 + value * (1.0 - sigma))


def encode(raw_rows, inst_rows, w_key_obs, w_val_obs, inst_table):
    obs_keys = jnp.dot(raw_rows, w_key_obs, preferred_element_type=jnp.float32).astype(jnp.bfloat16)
    inst_hot = (inst_rows[:, None] == lax.iota(jnp.int32, inst_table.shape[0])[None, :]).astype(
        jnp.bfloat16
    )
    pre_values = jnp.dot(raw_rows, w_val_obs, preferred_element_type=jnp.float32) + jnp.dot(
        inst_hot, inst_table, preferred_element_type=jnp.float32
    )
    obs_values = jax.nn.silu(pre_values).astype(jnp.bfloat16)
    return (obs_keys, obs_values, pre_values)


def times_transposed(left, weight):
    return lax.dot_general(
        left, weight, (((1,), (1,)), ((), ())), preferred_element_type=jnp.float32
    )


def rms_backward(resid_f, inverse, norm_gain, d_normed, cotangent_f):
    gained = norm_gain * d_normed
    return (
        cotangent_f
        + inverse * gained
        - resid_f * inverse**3 * jnp.mean(resid_f * gained, axis=-1, keepdims=True)
    )


def split_heads(rows, head_dim):
    return rows.reshape(rows.shape[0], rows.shape[1] // head_dim, head_dim)


def zonal_scores(q_heads, k_heads, v_heads, a_heads, score_scale):
    raw_score = (
        jnp.einsum("phd,lhd->hpl", q_heads, k_heads, preferred_element_type=jnp.float32)
        * score_scale
    )
    weight_z = jnp.exp(capped(raw_score))
    d_prob = jnp.einsum("phd,lhd->hpl", a_heads, v_heads, preferred_element_type=jnp.float32)
    return (raw_score, weight_z, d_prob)


def zonal_query_side(zq_rows, zk_all, zv_all, d_att, head_dim):
    score_scale = 1.0 / math.sqrt(head_dim)
    q_heads = split_heads(zq_rows, head_dim)
    k_heads = split_heads(zk_all, head_dim)
    a_heads = split_heads(d_att, head_dim)
    raw_score, weight_z, d_prob = zonal_scores(
        q_heads, k_heads, split_heads(zv_all, head_dim), a_heads, score_scale
    )
    row_total = jnp.sum(weight_z, axis=2, keepdims=True)
    prob_f = weight_z / row_total
    inner_sum = jnp.sum(prob_f * d_prob, axis=2, keepdims=True)
    d_raw = (prob_f * (d_prob - inner_sum) * cap_slope(raw_score) * score_scale).astype(
        jnp.bfloat16
    )
    d_query = (
        jnp.einsum("hpl,lhd->phd", d_raw, k_heads, preferred_element_type=jnp.float32)
        .astype(jnp.bfloat16)
        .reshape(zq_rows.shape[0], -1)
    )
    return (d_query, d_raw, prob_f, row_total[:, :, 0], inner_sum[:, :, 0], q_heads, a_heads)


def key_terms(d_raw, prob_f, q_heads, a_heads, count_k):
    prob_b = prob_f.astype(jnp.bfloat16)
    key_term = jnp.einsum(
        "hpl,phd->lhd", d_raw, q_heads, preferred_element_type=jnp.float32
    ).reshape(count_k, -1)
    value_term = jnp.einsum(
        "hpl,phd->lhd", prob_b, a_heads, preferred_element_type=jnp.float32
    ).reshape(count_k, -1)
    return (key_term, value_term)


def pad_row(rows):
    return jnp.concatenate([rows, jnp.zeros((1,) + rows.shape[1:], rows.dtype)], axis=0)


def on_device(
    tokens,
    cotangent,
    raw_obs,
    obs_band,
    obs_slot,
    obs_inst,
    obs_count,
    w_key_obs,
    w_val_obs,
    inst_table,
    null_key,
    null_val,
    w_query,
    norm_gain,
    zonal_query,
    zonal_key,
    zonal_value,
    zonal_out,
):
    model_width = tokens.shape[2]
    tok_rows = tokens.shape[1]
    head_count = model_width // HEAD_DIM
    score_scale = 1.0 / math.sqrt(HEAD_DIM)
    band_count = lax.axis_size("lat")
    obs_rows = raw_obs.shape[0]
    capacity = 2 * obs_rows // band_count
    slot_total = band_count * capacity
    resid_in = tokens.reshape(tok_rows, model_width)
    cotangent_rows = cotangent.reshape(tok_rows, model_width)
    obs_dest = obs_band[:, 0]
    row_order = lax.iota(jnp.int32, obs_rows)
    live_rows = row_order < obs_count[0]
    dest_hot = (
        (obs_dest[:, None] == lax.iota(jnp.int32, band_count)[None, :]) & live_rows[:, None]
    ).astype(jnp.bfloat16)
    earlier = (row_order[None, :] < row_order[:, None]).astype(jnp.bfloat16)
    before = jnp.dot(earlier, dest_hot, preferred_element_type=jnp.float32)
    rank_rows = jnp.sum(before * dest_hot.astype(jnp.float32), axis=1).astype(jnp.int32)
    position = jnp.where(live_rows, obs_dest * capacity + rank_rows, slot_total)

    def pack_rows(rows, fill_value):
        buffer = jnp.full((slot_total,) + rows.shape[1:], fill_value, rows.dtype)
        buffer = buffer.at[position].set(rows, mode="drop")
        return buffer.reshape((band_count, capacity) + rows.shape[1:])

    slot_buffer = pack_rows(obs_slot, tok_rows)
    obs_keys, obs_values, pre_values = encode(raw_obs, obs_inst, w_key_obs, w_val_obs, inst_table)
    key_recv, value_recv, slot_recv = (
        lax.all_to_all(pack_rows(obs_keys, 0.0), "lat", split_axis=0, concat_axis=0, tiled=True),
        lax.all_to_all(pack_rows(obs_values, 0.0), "lat", split_axis=0, concat_axis=0, tiled=True),
        lax.all_to_all(slot_buffer, "lat", split_axis=0, concat_axis=0, tiled=True),
    )
    key_slots = key_recv.reshape(slot_total, model_width)
    value_slots = value_recv.reshape(slot_total, model_width)
    slot_flat = slot_recv.reshape(slot_total)
    slot_live = slot_flat < tok_rows
    segments = tok_rows + 1
    query_rows = jnp.dot(resid_in, w_query, preferred_element_type=jnp.float32).astype(jnp.bfloat16)
    q_heads = query_rows.reshape(tok_rows, head_count, HEAD_DIM)
    q_slot = (
        jnp.take(pad_row(query_rows), slot_flat, axis=0)
        .astype(jnp.float32)
        .reshape(slot_total, head_count, HEAD_DIM)
    )
    k_heads = key_slots.astype(jnp.float32).reshape(slot_total, head_count, HEAD_DIM)
    v_heads = value_slots.astype(jnp.float32).reshape(slot_total, head_count, HEAD_DIM)
    null_k = null_key.astype(jnp.float32).reshape(head_count, HEAD_DIM)
    null_v = null_val.astype(jnp.float32).reshape(head_count, HEAD_DIM)
    raw_cross = jnp.sum(q_slot * k_heads, axis=2) * score_scale
    weight_cross = jnp.where(slot_live[:, None], jnp.exp(capped(raw_cross)), 0.0)
    raw_null = jnp.sum(q_heads.astype(jnp.float32) * null_k, axis=2) * score_scale
    weight_null = jnp.exp(capped(raw_null))
    total_cross = (
        weight_null + jax.ops.segment_sum(weight_cross, slot_flat, num_segments=segments)[:tok_rows]
    )
    total_pad = jnp.concatenate([total_cross, jnp.ones((1, head_count), jnp.float32)], axis=0)
    prob_cross = weight_cross / jnp.take(total_pad, slot_flat, axis=0)
    prob_null = weight_null / total_cross
    prob_cross_b = prob_cross.astype(jnp.bfloat16)
    prob_null_b = prob_null.astype(jnp.bfloat16)
    weighted = (prob_cross_b.astype(jnp.float32)[:, :, None] * v_heads).reshape(
        slot_total, model_width
    )
    gathered = jax.ops.segment_sum(weighted, slot_flat, num_segments=segments)[:tok_rows]
    gathered = gathered + (prob_null_b.astype(jnp.float32)[:, :, None] * null_v).reshape(
        tok_rows, model_width
    )
    resid_mid = (resid_in.astype(jnp.float32) + gathered).astype(jnp.bfloat16)
    resid_f = resid_mid.astype(jnp.float32)
    inverse = lax.rsqrt(jnp.mean(resid_f * resid_f, axis=1, keepdims=True) + norm_eps)
    normed = (resid_f * inverse * norm_gain).astype(jnp.bfloat16)
    zonal_q = jnp.dot(normed, zonal_query, preferred_element_type=jnp.float32).astype(jnp.bfloat16)
    zonal_k = jnp.dot(normed, zonal_key, preferred_element_type=jnp.float32).astype(jnp.bfloat16)
    zonal_v = jnp.dot(normed, zonal_value, preferred_element_type=jnp.float32).astype(jnp.bfloat16)
    key_whole, value_whole = (
        lax.all_gather(zonal_k, "lon", axis=0, tiled=True),
        lax.all_gather(zonal_v, "lon", axis=0, tiled=True),
    )
    d_att = times_transposed(cotangent_rows, zonal_out).astype(jnp.bfloat16)
    d_zq, d_zraw, zprob_f, row_total, inner_sum, zq_heads, att_heads = zonal_query_side(
        zonal_q, key_whole, value_whole, d_att, HEAD_DIM
    )
    key_term, value_term = key_terms(d_zraw, zprob_f, zq_heads, att_heads, key_whole.shape[0])
    d_zk, d_zv = (
        lax.psum_scatter(key_term, "lon", scatter_dimension=0, tiled=True),
        lax.psum_scatter(value_term, "lon", scatter_dimension=0, tiled=True),
    )
    d_normed = (
        times_transposed(d_zq, zonal_query)
        + times_transposed(d_zk.astype(jnp.bfloat16), zonal_key)
        + times_transposed(d_zv.astype(jnp.bfloat16), zonal_value)
    )
    d_resid = rms_backward(
        resid_f, inverse, norm_gain, d_normed, cotangent_rows.astype(jnp.float32)
    ).astype(jnp.bfloat16)
    d_heads = d_resid.astype(jnp.float32).reshape(tok_rows, head_count, HEAD_DIM)
    d_slot = (
        jnp.take(pad_row(d_resid), slot_flat, axis=0)
        .astype(jnp.float32)
        .reshape(slot_total, head_count, HEAD_DIM)
    )
    d_prob = jnp.sum(d_slot * v_heads, axis=2)
    d_prob_null = jnp.sum(d_heads * null_v, axis=2)
    inner_cross = (
        prob_null * d_prob_null
        + jax.ops.segment_sum(prob_cross * d_prob, slot_flat, num_segments=segments)[:tok_rows]
    )
    inner_pad = jnp.concatenate([inner_cross, jnp.zeros((1, head_count), jnp.float32)], axis=0)
    d_raw = (
        prob_cross
        * (d_prob - jnp.take(inner_pad, slot_flat, axis=0))
        * cap_slope(raw_cross)
        * score_scale
    ).astype(jnp.bfloat16)
    d_raw_null = prob_null * (d_prob_null - inner_cross) * cap_slope(raw_null) * score_scale
    d_raw_f = d_raw.astype(jnp.float32)
    d_query = jax.ops.segment_sum(
        (d_raw_f[:, :, None] * k_heads).reshape(slot_total, model_width),
        slot_flat,
        num_segments=segments,
    )[:tok_rows]
    d_query = (d_query + (d_raw_null[:, :, None] * null_k).reshape(tok_rows, model_width)).astype(
        jnp.bfloat16
    )
    d_tokens = (d_resid.astype(jnp.float32) + times_transposed(d_query, w_query)).astype(
        jnp.bfloat16
    )
    d_key_slots = (
        (d_raw_f[:, :, None] * q_slot).reshape(slot_total, model_width).astype(jnp.bfloat16)
    )
    d_value_slots = (
        (prob_cross_b.astype(jnp.float32)[:, :, None] * d_slot)
        .reshape(slot_total, model_width)
        .astype(jnp.bfloat16)
    )
    obs_norm = 1.0 / math.sqrt(obs_rows * band_count * lax.axis_size("lon"))
    key_back, value_back = (
        lax.all_to_all(
            d_key_slots.reshape(band_count, capacity, model_width),
            "lat",
            split_axis=0,
            concat_axis=0,
            tiled=True,
        ),
        lax.all_to_all(
            d_value_slots.reshape(band_count, capacity, model_width),
            "lat",
            split_axis=0,
            concat_axis=0,
            tiled=True,
        ),
    )
    d_key_rows = jnp.take(
        key_back.reshape(slot_total, model_width), position, axis=0, mode="fill", fill_value=0
    )
    d_value_rows = jnp.take(
        value_back.reshape(slot_total, model_width), position, axis=0, mode="fill", fill_value=0
    )
    d_pre = (d_value_rows.astype(jnp.float32) * silu_slope(pre_values)).astype(jnp.bfloat16)
    key_part = (
        lax.dot_general(
            raw_obs, d_key_rows, (((0,), (0,)), ((), ())), preferred_element_type=jnp.float32
        )
        * obs_norm
    )
    value_part = (
        lax.dot_general(
            raw_obs, d_pre, (((0,), (0,)), ((), ())), preferred_element_type=jnp.float32
        )
        * obs_norm
    )
    key_grad, value_grad = lax.psum((key_part, value_part), ("lat", "lon"))
    return (d_tokens.reshape(1, tok_rows, model_width), key_grad, value_grad)


def solution(mesh):
    return jax.shard_map(
        on_device,
        mesh=mesh,
        in_specs=(
            P("lat", "lon", None),
            P("lat", "lon", None),
            P(("lat", "lon"), None),
            P(("lat", "lon"), None),
            P(("lat", "lon")),
            P(("lat", "lon")),
            P(("lat", "lon")),
            P(),
            P(),
            P(),
            P(),
            P(),
            P(),
            P(),
            P(),
            P(),
            P(),
            P(),
        ),
        out_specs=(P("lat", "lon", None), P(), P()),
        check_vma=False,
    )
```

profile of v0, /device:TPU:1, one launch (start us, length us, event | category | flops | bytes accessed | tf_op | source)
XLA Modules:
  0.0 998.0 jit_solution(9869363092834164619)
XLA Ops:
  13.1 21.4 %all-to-all-start = ((s32[128,1,8]{2,1,0:T(1,128)}), s32[128,1,8]{2,1,0:T(1,128)S(1)}, u32[]{:S(2)}, u32[]{:S(2)}) async-start(s32[128,1,8]{2,1,0:T(1,128)} %bitcast.6), calls=%async_computation | async-start | bytes 131072 | tf_op jit(solution)/shard_map/all_to_all | solution.py:158
  35.8 3.7 scatter_custom_fusion.1
  39.5 8.4 all-to-all-done
  47.9 8.0 all-to-all-start.1
  57.8 4.8 scatter_custom_fusion.3
  62.6 53.9 %all-to-all-done.1 = bf16[128,8,640]{2,1,0:T(8,128)(2,1)S(1)} async-done(((bf16[128,8,640]{2,1,0:T(8,128)(2,1)}), bf16[128,8,640]{2,1,0:T(8,128)(2,1)S(1)}, u32[]{:S(2)}, u32[]{:S(2)}) %all-to-all-start.1) | async-done | bytes 1310752 | tf_op jit(solution)/shard_map/all_to_all | solution.py:156
  116.5 12.9 %all-to-all-start.2 = ((bf16[128,8,640]{2,1,0:T(8,128)(2,1)}), bf16[128,8,640]{2,1,0:T(8,128)(2,1)}, u32[]{:S(2)}, u32[]{:S(2)}) async-start(bf16[128,8,640]{2,1,0:T(8,128)(2,1)} %bitcast.91), calls=%async_computation.2 | async-start | bytes 2621440 | tf_op jit(solution)/shard_map/all_to_all | solution.py:157
  134.0 5.2 gather_fusion
  142.3 3.3 copy.99
  145.6 4.2 reshape.190
  149.8 6.7 copy.100
  159.1 6.0 scatter_custom_fusion.2
  174.0 15.4 %all-to-all-done.2 = bf16[128,8,640]{2,1,0:T(8,128)(2,1)} async-done(((bf16[128,8,640]{2,1,0:T(8,128)(2,1)}), bf16[128,8,640]{2,1,0:T(8,128)(2,1)}, u32[]{:S(2)}, u32[]{:S(2)}) %all-to-all-start.2) | async-done | bytes 1310752 | tf_op jit(solution)/shard_map/all_to_all | solution.py:157
  189.4 8.8 scatter_custom_fusion.4
  205.1 14.1 %all_gather.6 = bf16[512,640]{1,0:T(8,128)(2,1)S(1)} all-gather(bf16[128,640]{1,0:T(8,128)(2,1)S(1)} %convolution_convert_fusion.4), channel_id=1, replica_groups=mesh['lat'=128,'lon'=4] {'lon'}, dimensions={0}, use_global_device_ids=true | all-gather | bytes 819200 | tf_op jit(solution)/shard_map/all_gather | solution.py:203
  220.3 9.6 all_gather.7
  234.6 12.3 %fusion.13 = f32[10,64,512]{2,1,0:T(8,128)} fusion(bf16[128,10,64]{0,2,1:T(8,128)(2,1)S(1)} %bitcast.106, f32[10,128,512]{2,1,0:T(8,128)} %fusion.99, f32[10,128,512]{2,1,0:T(8,128)} %get-tuple-element.25, f32[10,128]{1,0:T(8,128)S(1)} %get-tuple-element.24), kind=kOutput, calls=%fused_computation.38 | convolution fusion | flops 93062912 | bytes 6722560 | tf_op jit(solution)/shard_map/hpl,phd->lhd/dot_general | solution.py:94
  247.5 3.9 fusion.10
  251.5 5.9 reshape.193
  257.4 6.8 copy.113
  264.2 11.1 %fusion.22 = bf16[10,64,128]{2,1,0:T(8,128)(2,1)S(1)} fusion(bf16[512,10,64]{0,2,1:T(8,128)(2,1)S(1)} %bitcast.101, f32[10,128,512]{2,1,0:T(8,128)} %fusion.99, f32[10,128,512]{2,1,0:T(8,128)} %get-tuple-element.25, f32[10,128]{1,0:T(8,128)S(1)} %get-tuple-element.24), kind=kOutput, calls=%fused_computation.55 | convolution fusion | flops 93144832 | bytes 6067200 | tf_op jit(solution)/shard_map/hpl,lhd->phd/dot_general | solution.py:85
  275.7 12.2 %reduce-scatter.3.cloned.1.call-done = f32[128,640]{0,1:T(8,128)} async-done(((f32[512,640]{0,1:T(8,128)}), f32[128,640]{0,1:T(8,128)}) %reduce-scatter.3.cloned.1.call-update) | async-done | bytes 327696 | tf_op jit(solution)/shard_map/reduce_scatter | solution.py:212
  289.2 50.4 %reduce-scatter.5.cloned.1.call-done = f32[128,640]{0,1:T(8,128)} async-done(((f32[512,640]{0,1:T(8,128)}), f32[128,640]{0,1:T(8,128)}) %reduce-scatter.5.cloned.1.call-update) | async-done | bytes 327696 | tf_op jit(solution)/shard_map/reduce_scatter | solution.py:213
  342.1 4.0 gather_fusion.2
  354.8 6.2 scatter_custom_fusion.5
  366.3 3.4 copy.119
  369.7 4.3 fusion.9
  373.9 77.4 %all_to_all.29 = bf16[128,8,640]{2,1,0:T(8,128)(2,1)S(1)} all-to-all(bf16[128,8,640]{2,1,0:T(8,128)(2,1)S(1)} %get-tuple-element.20), channel_id=1, replica_groups=mesh['lat'=128,'lon'=4] {'lat'}, dimensions={0} | all-to-all | bytes 2621440 | tf_op jit(solution)/shard_map/all_to_all | solution.py:272
  451.3 11.9 %all-to-all-start.3 = ((bf16[128,8,640]{2,1,0:T(8,128)(2,1)}), bf16[128,8,640]{2,1,0:T(8,128)(2,1)S(1)}, u32[]{:S(2)}, u32[]{:S(2)}) async-start(bf16[128,8,640]{2,1,0:T(8,128)(2,1)} %get-tuple-element.21), calls=%async_computation.5 | async-start | bytes 2621440 | tf_op jit(solution)/shard_map/all_to_all | solution.py:265
  465.9 8.9 scatter_custom_fusion.6
  477.6 46.0 %all-to-all-done.3 = bf16[128,8,640]{2,1,0:T(8,128)(2,1)S(1)} async-done(((bf16[128,8,640]{2,1,0:T(8,128)(2,1)}), bf16[128,8,640]{2,1,0:T(8,128)(2,1)S(1)}, u32[]{:S(2)}, u32[]{:S(2)}) %all-to-all-start.3) | async-done | bytes 1310752 | tf_op jit(solution)/shard_map/all_to_all | solution.py:265
  532.0 456.1 %all-reduce.7.cloned.1.call-done = (f32[64,640]{1,0:T(8,128)}, f32[64,640]{1,0:T(8,128)}) async-done(((f32[64,640]{1,0:T(8,128)}, f32[64,640]{1,0:T(8,128)}), (f32[64,640]{1,0:T(8,128)}, f32[64,640]{1,0:T(8,128)})) %all-reduce.7.cloned.1.call-update) | async-done | bytes 327696 | tf_op jit(solution)/shard_map/psum | solution.py:299
  (167 shorter events, 75.3 us)
Async XLA Ops:
  7.2 195.3 %copy-start = (bf16[640,640]{1,0:T(8,128)(2,1)S(1)}, bf16[640,640]{1,0:T(8,128)(2,1)}, u32[]{:S(2)}) copy-start(bf16[640,640]{1,0:T(8,128)(2,1)} %param.40) | copy-start | bytes 2457604
  9.0 46.9 %copy-start.29 = (bf16[32,640]{1,0:T(8,128)(2,1)S(1)}, bf16[32,640]{1,0:T(8,128)(2,1)}, u32[]{:S(2)}) copy-start(bf16[32,640]{1,0:T(8,128)(2,1)} %param.33) | copy-start | bytes 122884
  9.0 46.9 %copy-start.37 = (s32[512]{0:T(512)S(1)}, s32[512]{0:T(512)}, u32[]{:S(2)}) copy-start(s32[512]{0:T(512)} %param.29) | copy-start | bytes 6148
  13.1 34.8 %all-to-all-start = ((s32[128,1,8]{2,1,0:T(1,128)}), s32[128,1,8]{2,1,0:T(1,128)S(1)}, u32[]{:S(2)}, u32[]{:S(2)}) async-start(s32[128,1,8]{2,1,0:T(1,128)} %bitcast.6), calls=%async_computation | async-start | bytes 131072 | tf_op jit(solution)/shard_map/all_to_all | solution.py:158
  35.8 20.6 %copy-start.24 = (bf16[512,64]{0,1:T(8,128)(2,1)S(1)}, bf16[512,64]{0,1:T(8,128)(2,1)}, u32[]{:S(2)}) copy-start(bf16[512,64]{0,1:T(8,128)(2,1)} %param.26) | copy-start | bytes 196612
  35.8 20.6 %copy-start.27 = (bf16[64,640]{1,0:T(8,128)(2,1)S(1)}, bf16[64,640]{1,0:T(8,128)(2,1)}, u32[]{:S(2)}) copy-start(bf16[64,640]{1,0:T(8,128)(2,1)} %param.32) | copy-start | bytes 245764
  47.9 68.5 %all-to-all-start.1 = ((bf16[128,8,640]{2,1,0:T(8,128)(2,1)}), bf16[128,8,640]{2,1,0:T(8,128)(2,1)S(1)}, u32[]{:S(2)}, u32[]{:S(2)}) async-start(bf16[128,8,640]{2,1,0:T(8,128)(2,1)} %bitcast.92), calls=%async_computation.1 | async-start | bytes 2621440 | tf_op jit(solution)/shard_map/all_to_all | solution.py:156
  57.8 71.6 %copy-start.11 = (bf16[640,640]{1,0:T(8,128)(2,1)S(1)}, bf16[640,640]{1,0:T(8,128)(2,1)}, u32[]{:S(2)}) copy-start(bf16[640,640]{1,0:T(8,128)(2,1)} %param.36) | copy-start | bytes 2457604
  57.8 71.6 %copy-start.16 = (bf16[1,128,640]{2,1,0:T(8,128)(2,1)S(1)}, bf16[1,128,640]{2,1,0:T(8,128)(2,1)}, u32[]{:S(2)}) copy-start(bf16[1,128,640]{2,1,0:T(8,128)(2,1)} %param.24) | copy-start | bytes 491524
  62.6 67.4 %copy-start.30 = (bf16[640]{0:T(1024)(128)(2,1)S(1)}, bf16[640]{0:T(1024)(128)(2,1)}, u32[]{:S(2)}) copy-start(bf16[640]{0:T(1024)(128)(2,1)} %param.35) | copy-start | bytes 3844
  62.6 67.4 %copy-start.31 = (bf16[640]{0:T(1024)(128)(2,1)S(1)}, bf16[640]{0:T(1024)(128)(2,1)}, u32[]{:S(2)}) copy-start(bf16[640]{0:T(1024)(128)(2,1)} %param.34) | copy-start | bytes 3844
  62.6 67.5 %copy-start.19 = (bf16[1,128,640]{2,1,0:T(8,128)(2,1)S(1)}, bf16[1,128,640]{2,1,0:T(8,128)(2,1)}, u32[]{:S(2)}) copy-start(bf16[1,128,640]{2,1,0:T(8,128)(2,1)} %param.25) | copy-start | bytes 491524
  116.5 29.1 %copy-start.3 = (bf16[128,8,640]{2,1,0:T(8,128)(2,1)}, bf16[128,8,640]{2,1,0:T(8,128)(2,1)S(1)}, u32[]{:S(2)}) copy-start(bf16[128,8,640]{2,1,0:T(8,128)(2,1)S(1)} %all-to-all-done.1) | copy-start | bytes 3932164
  116.5 73.0 %all-to-all-start.2 = ((bf16[128,8,640]{2,1,0:T(8,128)(2,1)}), bf16[128,8,640]{2,1,0:T(8,128)(2,1)}, u32[]{:S(2)}, u32[]{:S(2)}) async-start(bf16[128,8,640]{2,1,0:T(8,128)(2,1)} %bitcast.91), calls=%async_computation.2 | async-start | bytes 2621440 | tf_op jit(solution)/shard_map/all_to_all | solution.py:157
  129.4 158.5 %reduce-scatter.3.cloned.1.call-start = ((), (), s32[]{:S(2)}) async-start(), calls=%async_computation.7 | async-start | bytes 1638400 | tf_op jit(solution)/shard_map/reduce_scatter | solution.py:212
  149.8 6.7 copy-start.5
  174.0 25.5 %copy-start.1 = (f32[1024,640]{1,0:T(8,128)}, f32[1024,640]{1,0:T(8,128)S(1)}, u32[]{:S(2)}) copy-start(f32[1024,640]{1,0:T(8,128)S(1)} %copy.106) | copy-start | bytes 7864324
  174.0 26.1 %copy-start.28 = (f32[640]{0:T(1024)S(1)}, f32[640]{0:T(1024)}, u32[]{:S(2)}) copy-start(f32[640]{0:T(1024)} %param.37) | copy-start | bytes 7684
  200.1 20.2 %copy-start.35 = (f32[128]{0:T(128)}, f32[128]{0:T(128)S(1)}, u32[]{:S(2)}) copy-start(f32[128]{0:T(128)S(1)} %get-tuple-element.23) | copy-start | bytes 1540
  203.8 26.4 %copy-start.21 = (bf16[128,640]{0,1:T(8,128)(2,1)S(1)}, bf16[128,640]{0,1:T(8,128)(2,1)}, u32[]{:S(2)}) copy-start(bf16[128,640]{0,1:T(8,128)(2,1)} %copy.110) | copy-start | bytes 491524
  220.3 12.0 %copy-start.26 = (bf16[128,640]{0,1:T(8,128)(2,1)S(1)}, bf16[128,640]{0,1:T(8,128)(2,1)}, u32[]{:S(2)}) copy-start(bf16[128,640]{0,1:T(8,128)(2,1)} %copy.109) | copy-start | bytes 491524
  247.0 92.6 %reduce-scatter.5.cloned.1.call-start = ((), (), s32[]{:S(2)}) async-start(), calls=%async_computation.8 | async-start | bytes 1638400 | tf_op jit(solution)/shard_map/reduce_scatter | solution.py:213
  257.4 6.8 copy-start.18
  264.2 11.1 %copy-start.9 = (bf16[640,640]{1,0:T(8,128)(2,1)S(1)}, bf16[640,640]{1,0:T(8,128)(2,1)}, u32[]{:S(2)}) copy-start(bf16[640,640]{1,0:T(8,128)(2,1)} %param.38) | copy-start | bytes 2457604
  275.2 64.4 %copy-start.7 = (bf16[128,640]{1,0:T(8,128)(2,1)S(1)}, bf16[128,640]{1,0:T(8,128)(2,1)}, u32[]{:S(2)}) copy-start(bf16[128,640]{1,0:T(8,128)(2,1)} %copy-done.6) | copy-start | bytes 491524
  275.3 65.9 %copy-start.20 = (bf16[1,128,640]{2,1,0:T(8,128)(2,1)S(1)}, bf16[1,128,640]{2,1,0:T(8,128)(2,1)}, u32[]{:S(2)}) copy-start(bf16[1,128,640]{2,1,0:T(8,128)(2,1)} %param.25) | copy-start | bytes 491524
  275.3 65.9 %copy-start.36 = (f32[128]{0:T(128)S(1)}, f32[128]{0:T(128)}, u32[]{:S(2)}) copy-start(f32[128]{0:T(128)} %copy-done.35) | copy-start | bytes 1540
  275.3 65.9 %copy-start.38 = (f32[128]{0:T(128)S(1)}, f32[128]{0:T(128)}, u32[]{:S(2)}) copy-start(f32[128]{0:T(128)} %get-tuple-element.22) | copy-start | bytes 1540
  373.9 89.3 %copy-start.32 = (s32[512,1]{0,1:T(1,128)S(1)}, s32[512,1]{0,1:T(1,128)}, u32[]{:S(2)}) copy-start(s32[512,1]{0,1:T(1,128)} %param.27) | copy-start | bytes 6148
  373.9 89.3 %copy-start.34 = (f32[512]{0:T(512)S(1)}, f32[512]{0:T(512)}, u32[]{:S(2)}) copy-start(f32[512]{0:T(512)} %copy-done.33) | copy-start | bytes 6148
  451.3 72.2 %all-to-all-start.3 = ((bf16[128,8,640]{2,1,0:T(8,128)(2,1)}), bf16[128,8,640]{2,1,0:T(8,128)(2,1)S(1)}, u32[]{:S(2)}, u32[]{:S(2)}) async-start(bf16[128,8,640]{2,1,0:T(8,128)(2,1)} %get-tuple-element.21), calls=%async_computation.5 | async-start | bytes 2621440 | tf_op jit(solution)/shard_map/all_to_all | solution.py:265
  463.2 524.9 %all-reduce.7.cloned.1.call-start = ((), (), s32[]{:S(2)}) async-start(), calls=%async_computation.9 | async-start | bytes 655360 | tf_op jit(solution)/shard_map/psum | solution.py:299
  (14 other events, 39.1 us)
Sparse Core Ops, SparseCore 0:
  247.1 40.6 reduce-scatter.2
  291.2 48.3 reduce-scatter.4
  530.1 458.0 all-reduce.6
where the time goes:
time: 1010 us; the launch traced here: 998 us
  waiting for transfers between devices  642 us (64%)
  blocking collectives  101 us (10%)
  local copies, waits for them, and re-layouts  79.4 us (8%)
  starting transfers between devices  54.8 us (5%)
  other arithmetic  54.2 us (5%)
  matrix products  50.6 us (5%)
  between operations  15.4 us (2%)
    psum x1, waiting for transfers between devices, on_device(): key_grad, value_grad = lax.psum((key_part, value_part), ('lat', 'lon'))  456 us
    all_to_all x1, blocking collectives, on_device(): lax.all_to_all(d_value_slots.reshape(band_count, capacity, model_width),...  77.4 us
    all_to_all x1, waiting for transfers between devices, on_device(): lax.all_to_all(pack_rows(obs_keys, 0.0), 'lat', split_axis=0, concat_axis...  53.9 us
    reduce_scatter x1, waiting for transfers between devices, on_device(): lax.psum_scatter(value_term, 'lon', scatter_dimension=0, tiled=True)  50.4 us
    all_to_all x1, waiting for transfers between devices, on_device(): lax.all_to_all(d_key_slots.reshape(band_count, capacity, model_width), 'l...  46 us
    all_to_all x1, starting transfers between devices, on_device(): lax.all_to_all(slot_buffer, 'lat', split_axis=0, concat_axis=0, tiled=True)  21.4 us
  transfers between devices with their start and end apart: 7, of which 7 were waited for; matrix products, arithmetic and copies ran while one was open for 10% of the time, Pallas kernels for 0%

commit v1 on v0

v1 whole, which is shorter than its diff:
```python
import math

import jax
import jax.numpy as jnp
from jax import lax
from jax.experimental import pallas as pl
from jax.experimental.pallas import tpu as pltpu
from jax.sharding import PartitionSpec as P

HEAD_DIM = 64
CAP_ROWS = 8
LANES = 128
FEATS = 64

logit_cap = 6.0
norm_eps = 1e-06
score_scale = 1.0 / math.sqrt(HEAD_DIM)

bf16 = jnp.bfloat16
f32 = jnp.float32
i32 = jnp.int32

PLANE = 32
DEPTH = 16
CHUNK = 24
ROW_BLOCK = 256


def iota(shape, dim):
    return lax.broadcasted_iota(i32, shape, dim)


def dot_nn(a, b):
    return lax.dot_general(a, b, (((1,), (0,)), ((), ())), preferred_element_type=f32)


def dot_nt(a, b):
    return lax.dot_general(a, b, (((1,), (1,)), ((), ())), preferred_element_type=f32)


def dot_tn(a, b):
    return lax.dot_general(a, b, (((0,), (0,)), ((), ())), preferred_element_type=f32)


def halves(value):
    high = value.astype(bf16)
    return high, (value - high.astype(f32)).astype(bf16)


def fine_nn(a, value):
    high, low = halves(value)
    return dot_nn(a, high) + dot_nn(a, low)


def fine_tn(a, value):
    high, low = halves(value)
    return dot_tn(a, high) + dot_tn(a, low)


def head_sum_matrix(width):
    return jnp.where(
        iota((width, LANES), 0) // HEAD_DIM == iota((width, LANES), 1), 1.0, 0.0
    ).astype(bf16)


def head_spread_matrix(width):
    return jnp.where(
        iota((LANES, width), 1) // HEAD_DIM == iota((LANES, width), 0), 1.0, 0.0
    ).astype(bf16)


def token_hot(x_rows):
    slot = x_rows[:, FEATS : FEATS + 1].astype(f32).astype(i32)
    return jnp.where(iota((x_rows.shape[0], LANES), 1) == slot - 1, 1.0, 0.0).astype(bf16)


def pack_kernel(count_ref, band_ref, slot_ref, inst_ref, raw_ref, out_ref):
    rows = band_ref.shape[1]
    slots = out_ref.shape[0]
    bands = slots // CAP_ROWS
    band = band_ref[...]
    live = iota((1, rows), 1) < count_ref[0]
    dest = jnp.where(live, band, -1)
    named = iota((bands, rows), 0) == dest
    hot = jnp.where(named, 1.0, 0.0).astype(bf16)
    earlier = jnp.where(iota((rows, rows), 0) < iota((rows, rows), 1), 1.0, 0.0).astype(bf16)
    before = dot_nn(hot, earlier)
    rank = jnp.sum(jnp.where(named, before, 0.0), axis=0, keepdims=True).astype(i32)
    position = jnp.where(live, band * CAP_ROWS + rank, -1)
    pick = jnp.where(iota((slots, rows), 0) == position, 1.0, 0.0).astype(bf16)
    part = iota((LANES - FEATS, rows), 0)
    meta = jnp.where(
        part == 0,
        (slot_ref[...] + 1).astype(f32),
        jnp.where(part == 1, inst_ref[...].astype(f32), 0.0),
    ).astype(bf16)
    payload = jnp.concatenate([raw_ref[...], meta], axis=0)
    out_ref[...] = dot_nt(pick, payload).astype(bf16)


def cross_kernel(
    x_ref,
    query_ref,
    tok_ref,
    wk_ref,
    wv_ref,
    table_ref,
    nk_ref,
    nv_ref,
    gain_ref,
    resid_ref,
    normed_ref,
    key_ref,
    val_ref,
    slope_ref,
    qs_ref,
    tanh_ref,
    prob_ref,
    ntanh_ref,
    nprob_ref,
    hot_s,
    weight_s,
):
    slots = x_ref.shape[0]
    toks, width = tok_ref.shape
    pad = jnp.zeros((LANES - FEATS, width), bf16)
    w_key = jnp.concatenate([wk_ref[...], pad], axis=0)
    w_val = jnp.concatenate(
        [wv_ref[...], pad, table_ref[...], jnp.zeros((LANES - table_ref.shape[0], width), bf16)],
        axis=0,
    )
    head_sum = head_sum_matrix(width)
    head_spread = head_spread_matrix(width)
    query = query_ref[...]
    total = jnp.zeros((toks, LANES), f32)
    for start in range(0, slots, ROW_BLOCK):
        span = pl.ds(start, ROW_BLOCK)
        x = x_ref[span, :]
        hot = token_hot(x)
        hot_s[span, :] = hot
        inst = x[:, FEATS + 1 : FEATS + 2].astype(f32).astype(i32)
        inst_hot = jnp.where(iota((ROW_BLOCK, LANES), 1) == inst, 1.0, 0.0).astype(bf16)
        keys = dot_nn(x, w_key).astype(bf16)
        key_ref[span, :] = keys
        pre = dot_nn(jnp.concatenate([x, inst_hot], axis=1), w_val)
        sigma = 1.0 / (1.0 + jnp.exp(-pre))
        val_ref[span, :] = (pre * sigma).astype(bf16)
        slope_ref[span, :] = (sigma * (1.0 + pre * (1.0 - sigma))).astype(bf16)
        q_slot = dot_nn(hot, query).astype(bf16)
        qs_ref[span, :] = q_slot
        t = jnp.tanh(dot_nn(q_slot * keys, head_sum) * (score_scale / logit_cap))
        tanh_ref[span, :] = t
        weight = jnp.exp(logit_cap * t)
        weight_s[span, :] = weight
        total = total + fine_tn(hot, weight)
    null_t = jnp.tanh(
        fine_nn_left(query.astype(f32) * nk_ref[...].astype(f32), head_sum)
        * (score_scale / logit_cap)
    )
    null_weight = jnp.exp(logit_cap * null_t)
    share = 1.0 / (total + null_weight)
    null_prob = null_weight * share
    ntanh_ref[...] = null_t
    nprob_ref[...] = null_prob
    gathered = dot_nn(null_prob.astype(bf16), head_spread) * nv_ref[...].astype(f32)
    for start in range(0, slots, ROW_BLOCK):
        span = pl.ds(start, ROW_BLOCK)
        hot = hot_s[span, :]
        prob = weight_s[span, :] * fine_nn(hot, share)
        prob_ref[span, :] = prob
        spread = dot_nn(prob.astype(bf16), head_spread).astype(bf16)
        gathered = gathered + dot_tn(hot, spread * val_ref[span, :])
    resid = (tok_ref[...].astype(f32) + gathered).astype(bf16)
    resid_ref[...] = resid
    resid_f = resid.astype(f32)
    inverse = lax.rsqrt(jnp.mean(resid_f * resid_f, axis=1, keepdims=True) + norm_eps)
    normed_ref[...] = (resid_f * inverse * gain_ref[...]).astype(bf16)


def fine_nn_left(value, b):
    high, low = halves(value)
    return dot_nn(high, b) + dot_nn(low, b)


def zonal_kernel(
    me_ref,
    normed_ref,
    att_ref,
    zq_ref,
    zk_ref,
    zv_ref,
    resid_ref,
    cot_ref,
    gain_ref,
    dres_ref,
    zq_s,
    zk_s,
    zkt_s,
    zv_s,
    att_s,
    norm_s,
    dq_s,
    dk_s,
    dv_s,
):
    whole, width = normed_ref.shape
    own = resid_ref.shape[0]
    sectors = whole // own
    pairs = width // LANES
    me = me_ref[0]
    for k in range(sectors):
        src = pl.multiple_of(lax.rem(me + k, sectors) * own, own)
        norm_s[k * own : (k + 1) * own, :] = normed_ref[pl.ds(src, own), :]
        part = att_ref[pl.ds(src, own), :]
        for p in range(pairs):
            att_s[p, k * own : (k + 1) * own, :] = part[:, p * LANES : (p + 1) * LANES]
    normed = norm_s[...]
    for ref, out in ((zq_ref, zq_s), (zk_ref, zk_s), (zv_ref, zv_s)):
        proj = dot_nn(normed, ref[...])
        for p in range(pairs):
            piece = proj[:, p * LANES : (p + 1) * LANES]
            out[p] = piece.astype(bf16)
            if out is zk_s:
                zkt_s[p] = piece.T.astype(bf16)
    lane_head = iota((whole, LANES), 1) // HEAD_DIM
    step = 2 * own

    def one_pair(p, carry):
        keys = zk_s[p]
        vals = zv_s[p]
        dk = jnp.zeros((own, LANES), f32)
        dv = jnp.zeros((own, LANES), f32)
        for head in range(2):
            qm = jnp.where(lane_head == head, zq_s[p], jnp.zeros((), bf16))
            am = jnp.where(lane_head == head, att_s[p], jnp.zeros((), bf16))
            for start in range(0, whole, step):
                q_part = qm[start : start + step]
                a_part = am[start : start + step]
                t = jnp.tanh(dot_nt(keys, q_part) * (score_scale / logit_cap))
                zdp = dot_nt(vals, a_part)
                weight = jnp.exp(logit_cap * t)
                share = 1.0 / jnp.sum(weight, axis=0, keepdims=True)
                inner = jnp.sum(weight * zdp, axis=0, keepdims=True) * share
                scaled = share * score_scale

                def d_raw_of(rows, cols):
                    tt = t[rows, cols]
                    return (
                        weight[rows, cols]
                        * scaled[:, cols]
                        * (zdp[rows, cols] - inner[:, cols])
                        * (1.0 - tt * tt)
                    ).astype(bf16)

                top = d_raw_of(slice(0, own), slice(None))
                prob = (weight[:own] * share).astype(bf16)
                dk = dk + dot_nn(top, q_part)
                dv = dv + dot_nn(prob, a_part)
                if start == 0:
                    rest = d_raw_of(slice(own, None), slice(0, own))
                    column = jnp.concatenate([top[:, :own], rest], axis=0)
                    keys_t = zkt_s[p, head * HEAD_DIM : (head + 1) * HEAD_DIM, :]
                    dq_s[p, head * HEAD_DIM : (head + 1) * HEAD_DIM, :] = dot_nn(keys_t, column)
        dk_s[p] = dk.astype(bf16)
        dv_s[p] = dv.astype(bf16)
        return carry

    lax.fori_loop(0, pairs, one_pair, 0)
    d_normed = jnp.zeros((own, width), f32)
    for p in range(pairs):
        cols = slice(p * LANES, (p + 1) * LANES)
        d_normed = d_normed + dot_nt(dq_s[p].T.astype(bf16), zq_ref[:, cols])
        d_normed = d_normed + dot_nt(dk_s[p], zk_ref[:, cols])
        d_normed = d_normed + dot_nt(dv_s[p], zv_ref[:, cols])
    resid_f = resid_ref[...].astype(f32)
    inverse = lax.rsqrt(jnp.mean(resid_f * resid_f, axis=1, keepdims=True) + norm_eps)
    gained = gain_ref[...] * d_normed
    dres_ref[...] = (
        cot_ref[...].astype(f32)
        + inverse * gained
        - resid_f * (inverse * inverse * inverse) * jnp.mean(resid_f * gained, axis=1, keepdims=True)
    ).astype(bf16)


def back_kernel(
    x_ref,
    dres_ref,
    wq_ref,
    nk_ref,
    nv_ref,
    key_ref,
    val_ref,
    slope_ref,
    qs_ref,
    tanh_ref,
    prob_ref,
    ntanh_ref,
    nprob_ref,
    dtok_ref,
    grad_ref,
    ds_s,
    dp_s,
):
    slots = x_ref.shape[0]
    toks, width = dres_ref.shape
    head_sum = head_sum_matrix(width)
    head_spread = head_spread_matrix(width)
    d_resid = dres_ref[...]
    null_prob = nprob_ref[...]
    null_t = ntanh_ref[...]
    null_dp = fine_nn_left(d_resid.astype(f32) * nv_ref[...].astype(f32), head_sum)
    inner = null_prob * null_dp
    for start in range(0, slots, ROW_BLOCK):
        span = pl.ds(start, ROW_BLOCK)
        hot = token_hot(x_ref[span, :])
        d_slot = dot_nn(hot, d_resid).astype(bf16)
        ds_s[span, :] = d_slot
        dp = dot_nn(d_slot * val_ref[span, :], head_sum)
        dp_s[span, :] = dp
        inner = inner + fine_tn(hot, prob_ref[span, :] * dp)
    null_raw = null_prob * (null_dp - inner) * (1.0 - null_t * null_t) * score_scale
    d_query = fine_nn_left(null_raw, head_spread) * nk_ref[...].astype(f32)
    grads = jnp.zeros((LANES, 2 * width), f32)
    for start in range(0, slots, ROW_BLOCK):
        span = pl.ds(start, ROW_BLOCK)
        x = x_ref[span, :]
        hot = token_hot(x)
        prob = prob_ref[span, :]
        t = tanh_ref[span, :]
        d_raw = (
            prob * (dp_s[span, :] - fine_nn(hot, inner)) * (1.0 - t * t) * score_scale
        ).astype(bf16)
        d_raw_wide = dot_nn(d_raw, head_spread).astype(bf16)
        prob_wide = dot_nn(prob.astype(bf16), head_spread).astype(bf16)
        d_query = d_query + dot_tn(hot, d_raw_wide * key_ref[span, :])
        d_keys = d_raw_wide * qs_ref[span, :]
        d_pre = (prob_wide * ds_s[span, :]) * slope_ref[span, :]
        grads = grads + dot_tn(x, jnp.concatenate([d_keys, d_pre], axis=1))
    d_tok = d_resid.astype(f32) + dot_nt(d_query.astype(bf16), wq_ref[...])
    dtok_ref[...] = d_tok.astype(bf16)
    blocks = 2 * width // LANES
    for b in range(blocks):
        grad_ref[b * FEATS : (b + 1) * FEATS, :] = grads[
            :FEATS, b * LANES : (b + 1) * LANES
        ].astype(bf16)
    spare = grad_ref.shape[0] - blocks * FEATS
    grad_ref[blocks * FEATS :, :] = jnp.zeros((spare, LANES), bf16)


def whole_call(kernel, name, out_shape, args, scalars=0, scratch=()):
    vmem = pl.BlockSpec(memory_space=pltpu.VMEM)
    smem = pl.BlockSpec(memory_space=pltpu.SMEM)
    return pl.pallas_call(
        kernel,
        name=name,
        out_shape=out_shape,
        in_specs=[smem] * scalars + [vmem] * (len(args) - scalars),
        out_specs=[vmem] * len(out_shape) if isinstance(out_shape, (list, tuple)) else vmem,
        scratch_shapes=list(scratch),
        compiler_params=pltpu.CompilerParams(vmem_limit_bytes=56 * 1024 * 1024),
    )(*args)


def shaped(rows, cols, dtype):
    return jax.ShapeDtypeStruct((rows, cols), dtype)


def pack(obs_count, obs_band, obs_slot, obs_inst, raw_obs, bands):
    rows = raw_obs.shape[0]
    return whole_call(
        pack_kernel,
        "pack",
        shaped(bands * CAP_ROWS, LANES, bf16),
        (
            obs_count,
            obs_band.reshape(1, rows),
            obs_slot.reshape(1, rows),
            obs_inst.reshape(1, rows),
            raw_obs.T,
        ),
        scalars=1,
    )


def cross_forward(x, query, tok, w_key, w_val, table, null_key, null_val, gain):
    slots = x.shape[0]
    toks, width = tok.shape
    big = shaped(slots, width, bf16)
    small = shaped(slots, LANES, f32)
    null = shaped(toks, LANES, f32)
    row = shaped(toks, width, bf16)
    return whole_call(
        cross_kernel,
        "cross_forward",
        [row, row, big, big, big, big, small, small, null, null],
        (x, query, tok, w_key, w_val, table, null_key, null_val, gain),
        scratch=(pltpu.VMEM((slots, LANES), bf16), pltpu.VMEM((slots, LANES), f32)),
    )


def zonal(me, normed_all, att_all, zq, zk, zv, resid, cot, gain):
    own, width = resid.shape
    whole = normed_all.shape[0]
    pairs = width // LANES
    rows = pltpu.VMEM((pairs, whole, LANES), bf16)
    return whole_call(
        zonal_kernel,
        "zonal",
        shaped(own, width, bf16),
        (me, normed_all, att_all, zq, zk, zv, resid, cot, gain),
        scalars=1,
        scratch=(
            rows,
            rows,
            pltpu.VMEM((pairs, LANES, whole), bf16),
            rows,
            rows,
            pltpu.VMEM((whole, width), bf16),
            pltpu.VMEM((pairs, LANES, own), f32),
            pltpu.VMEM((pairs, own, LANES), bf16),
            pltpu.VMEM((pairs, own, LANES), bf16),
        ),
    )


def cross_backward(x, d_resid, w_query, null_key, null_val, saved):
    slots = x.shape[0]
    toks, width = d_resid.shape
    return whole_call(
        back_kernel,
        "cross_backward",
        [shaped(toks, width, bf16), shaped(PLANE * CHUNK, LANES, bf16)],
        (x, d_resid, w_query, null_key, null_val) + tuple(saved),
        scratch=(pltpu.VMEM((slots, width), bf16), pltpu.VMEM((slots, LANES), f32)),
    )


def sum_everywhere(rows):
    plane = [list(range(z * PLANE, (z + 1) * PLANE)) for z in range(DEPTH)]
    lats = PLANE // 4
    column = [[z * lats + k for z in range(DEPTH)] for k in range(lats)]

    def swap(parts, axes, groups):
        return lax.all_to_all(
            parts, axes, split_axis=0, concat_axis=0, tiled=True, axis_index_groups=groups
        )

    def total(parts):
        return jnp.sum(parts.astype(f32), axis=0)

    parts = swap(rows.reshape(PLANE, CHUNK, LANES), ("lat", "lon"), plane)
    mine = total(parts).astype(bf16)
    parts = swap(jnp.broadcast_to(mine, (DEPTH, CHUNK, LANES)), "lat", column)
    mine = total(parts).astype(bf16)
    parts = swap(jnp.broadcast_to(mine, (PLANE, CHUNK, LANES)), ("lat", "lon"), plane)
    return parts.reshape(PLANE * CHUNK, LANES)


def on_device(
    tokens,
    cotangent,
    raw_obs,
    obs_band,
    obs_slot,
    obs_inst,
    obs_count,
    w_key_obs,
    w_val_obs,
    inst_table,
    null_key,
    null_val,
    w_query,
    norm_gain,
    zonal_query,
    zonal_key,
    zonal_value,
    zonal_out,
):
    tok_rows, width = tokens.shape[1:]
    bands = lax.axis_size("lat")
    devices = bands * lax.axis_size("lon")
    obs_total = raw_obs.shape[0] * devices
    tok = tokens.reshape(tok_rows, width)
    cot = cotangent.reshape(tok_rows, width)
    null_key = null_key.reshape(1, width)
    null_val = null_val.reshape(1, width)
    gain = norm_gain.reshape(1, width)
    packed = pack(obs_count, obs_band, obs_slot, obs_inst, raw_obs, bands)
    received = lax.all_to_all(
        packed.reshape(bands, CAP_ROWS, LANES), "lat", split_axis=0, concat_axis=0, tiled=True
    ).reshape(bands * CAP_ROWS, LANES)
    query = jnp.dot(tok, w_query, preferred_element_type=f32).astype(bf16)
    d_att = dot_nt(cot, zonal_out).astype(bf16)
    att_all = lax.all_gather(d_att, "lon", axis=0, tiled=True)
    resid, normed, *saved = cross_forward(
        received, query, tok, w_key_obs, w_val_obs, inst_table, null_key, null_val, gain
    )
    normed_all = lax.all_gather(normed, "lon", axis=0, tiled=True)
    me = lax.axis_index("lon").astype(i32).reshape(1)
    d_resid = zonal(
        me, normed_all, att_all, zonal_query, zonal_key, zonal_value, resid, cot, gain
    )
    d_tok, grads = cross_backward(received, d_resid, w_query, null_key, null_val, saved)
    summed = sum_everywhere(grads)[: 2 * FEATS * width // LANES]
    summed = summed.astype(f32) * (1.0 / math.sqrt(obs_total))
    summed = summed.reshape(2, width // LANES, FEATS, LANES).transpose(0, 2, 1, 3)
    summed = summed.reshape(2, FEATS, width)
    return d_tok.reshape(1, tok_rows, width), summed[0], summed[1]


def solution(mesh):
    return jax.shard_map(
        on_device,
        mesh=mesh,
        in_specs=(
            P("lat", "lon", None),
            P("lat", "lon", None),
            P(("lat", "lon"), None),
            P(("lat", "lon"), None),
            P(("lat", "lon")),
            P(("lat", "lon")),
            P(("lat", "lon")),
            P(),
            P(),
            P(),
            P(),
            P(),
            P(),
            P(),
            P(),
            P(),
            P(),
            P(),
        ),
        out_specs=(P("lat", "lon", None), P(), P()),
        check_vma=False,
    )
```

time: 1010 us -> 136 us (0.13); the launches traced: 998 us -> 136 us
  waiting for transfers between devices: 642 us -> 0.01 us
  local copies, waits for them, and re-layouts: 79.4 us -> 5.58 us
  other arithmetic: 54.2 us -> 0.09 us
  matrix products: 50.6 us -> 2.26 us
  starting transfers between devices: 54.8 us -> 21.6 us
  Pallas kernels: 0 us -> 32.4 us
  blocking collectives: 101 us -> 72.5 us
  between operations: 15.4 us -> 1.44 us
    psum x1 -> x0, waiting for transfers between devices: 456 us -> none  [on_device(): key_grad, value_grad = lax.psum((key_part, value_part), ('lat', 'lon'))]
    all_to_all x4 -> x1, waiting for transfers between devices: 124 us -> 0.01 us  [on_device(): lax.all_to_all(packed.reshape(bands, CAP_ROWS, LANES), 'lat', split_axis=...]
    reduce_scatter x2 -> x0, waiting for transfers between devices: 62.6 us -> none  [the longest x1 50.4 us: on_device(): lax.psum_scatter(value_term, 'lon', scatter_dimension=0, tiled=True)]
    dot_general x20 -> x2, matrix products: 50.6 us -> 2.26 us  [the longest x1 1.28 us: dot_nt(): lax.dot_general(a, b, (((1,), (1,)), ((), ())), preferred_element_type=f32)]
    all_to_all x4 -> x1, starting transfers between devices: 54.2 us -> 21.6 us  [on_device(): lax.all_to_all(packed.reshape(bands, CAP_ROWS, LANES), 'lat', split_axis=...]
    pallas_call x0 -> x4, Pallas kernels: none -> 32.4 us  [whole_call(): pl.pallas_call(kernel, name=name, out_shape=out_shape, in_specs=[smem] *...]
    convert_element_type x10 -> x0, local copies, waits for them, and re-layouts: 32.1 us -> none  [the longest x2 12.7 us: on_device(): value_slots.astype(jnp.float32).reshape(slot_total, head_count, HEAD_DIM)]
    all_to_all x1 -> x3, blocking collectives: 77.4 us -> 47.3 us  [swap(): lax.all_to_all(parts, axes, split_axis=0, concat_axis=0, tiled=True, axis...]
  transfers between devices with their start and end apart: 7 -> 1, of which waited for: 7 -> 0; matrix products, arithmetic and copies ran while one was open for 10% -> 4% of each run, Pallas kernels for 0% -> 0%
where the time goes in v1:
time: 136 us
  blocking collectives  72.5 us (53%)
  Pallas kernels  32.4 us (24%)
  starting transfers between devices  21.6 us (16%)
  local copies, waits for them, and re-layouts  5.58 us (4%)
  matrix products  2.26 us (2%)
  between operations  1.44 us (1%)
    all_to_all x3, blocking collectives, swap(): lax.all_to_all(parts, axes, split_axis=0, concat_axis=0, tiled=True, axis...  47.3 us
    pallas_call x4, Pallas kernels, whole_call(): pl.pallas_call(kernel, name=name, out_shape=out_shape, in_specs=[smem] *...  32.4 us
    all_to_all x1, starting transfers between devices, on_device(): lax.all_to_all(packed.reshape(bands, CAP_ROWS, LANES), 'lat', split_axis=...  21.6 us
    all_gather x1, blocking collectives, on_device(): normed_all = lax.all_gather(normed, 'lon', axis=0, tiled=True)  13.6 us
    all_gather x1, blocking collectives, on_device(): att_all = lax.all_gather(d_att, 'lon', axis=0, tiled=True)  11.6 us
  transfers between devices with their start and end apart: 1, of which 0 were waited for; matrix products, arithmetic and copies ran while one was open for 4% of the time, Pallas kernels for 0%

profile of v1, /device:TPU:1, one launch (start us, length us, event | category | flops | bytes accessed | tf_op | source)
XLA Modules:
  0.0 135.9 jit_solution(13634135838719585590)
XLA Ops:
  0.6 0.0 copy-start
  1.4 2.2 %pack.1 = bf16[1024,128]{1,0:T(8,128)(2,1)} custom-call(s32[1]{0:T(128)S(6)} %copy.29.count_ref, s32[1,512]{1,0:T(1,128)} %bitcast.40, s32[1,512]{1,0:T(1,128)} %bitcast.41, s32[1,512]{1,0:T(1,128)} %bitcast.42, bf16[64,512]{1,0:T(8,128)(2,1)} %bitcast.39), custom_call_target="tpu_custom_call" | custom-call | tf_op jit(solution)/shard_map/pack/pallas_call | solution.py:353
  3.6 0.0 copy-start.1
  3.6 0.0 copy-start.3
  3.6 21.6 %all-to-all-start = ((bf16[128,8,128]{2,1,0:T(8,128)(2,1)}), bf16[128,8,128]{2,1,0:T(8,128)(2,1)S(1)}, u32[]{:S(2)}, u32[]{:S(2)}) async-start(bf16[128,8,128]{2,1,0:T(8,128)(2,1)} %bitcast.32), calls=%async_computation | async-start | bytes 524288 | tf_op jit(solution)/shard_map/all_to_all | solution.py:489
  25.2 1.3 reshape.63.nk_ref
  26.5 1.3 reshape.64.nv_ref
  27.7 1.3 reshape.65.gain_ref
  29.0 0.0 copy-done
  29.0 1.3 convolution_convert_fusion
  30.3 11.6 %all_gather.7.att_ref = bf16[512,640]{1,0:T(8,128)(2,1)} all-gather(bf16[128,640]{1,0:T(8,128)(2,1)S(1)} %convolution_convert_fusion), channel_id=1, replica_groups=mesh['lat'=128,'lon'=4] {'lon'}, dimensions={0}, use_global_device_ids=true | all-gather | bytes 819200 | tf_op jit(solution)/shard_map/all_gather | solution.py:494
  41.9 0.0 copy-done.1
  41.9 0.0 copy-done.3
  41.9 1.0 convolution_convert_fusion.1.query_ref
  42.9 0.0 all-to-all-done
  42.9 0.0 copy-start.2
  42.9 0.7 copy-done.2
  43.6 7.5 %cross_forward.1 = (bf16[128,640]{1,0:T(8,128)(2,1)}, bf16[128,640]{1,0:T(8,128)(2,1)}, bf16[1024,640]{1,0:T(8,128)(2,1)}, bf16[1024,640]{1,0:T(8,128)(2,1)}, bf...) custom-call(bf16[1024,128]{1,0:T(8,128)(2,1)} %bitcast.29, ...), custom_call_target="tpu_custom_call" | custom-call | tf_op jit(solution)/shard_map/cross_forward/pallas_call | solution.py:353
  51.1 13.6 %all_gather.6.normed_ref = bf16[512,640]{1,0:T(8,128)(2,1)} all-gather(bf16[128,640]{1,0:T(8,128)(2,1)} %get-tuple-element.15), channel_id=1, replica_groups=mesh['lat'=128,'lon'=4] {'lon'}, dimensions={0}, use_global_device_ids=true | all-gather | bytes 819200 | tf_op jit(solution)/shard_map/all_gather | solution.py:498
  64.7 14.5 %zonal.1.dres_ref = bf16[128,640]{1,0:T(8,128)(2,1)} custom-call(s32[1]{0:T(128)} %bitcast.6.me_ref, bf16[512,640]{1,0:T(8,128)(2,1)} %all_gather.6.normed_ref, bf16[512,640]{1,0:T(8,128)(2,1)} %all_gather.7.att_ref, bf16[640,640]{1,0:T(8,128)(2,1)} %zq_ref.1, bf16[640,640]{1,0:T(8,128)(2,1)} %zk_ref.1, bf16[640,640]{1,0:T(8,128)(2,1)} %zv_ref.1, ...), custom_call_target="tpu_custom_call" | custom-call | tf_op jit(solution)/shard_map/zonal/pallas_call | solution.py:353
  79.2 8.2 %cross_backward.1 = (bf16[128,640]{1,0:T(8,128)(2,1)}, bf16[768,128]{1,0:T(8,128)(2,1)}) custom-call(bf16[1024,128]{1,0:T(8,128)(2,1)} %bitcast.30, bf16[128,640]{1,0:T(8,128)(2,1)} %zonal.1.dres_ref, bf16[640,640]{1,0:T(8,128)(2,1)} %wq_ref.1, bf16[1,640]{1,0:T(2,128)(2,1)} %reshape.63.nk_ref, bf16[1,640]{1,0:T(2,128)(2,1)} %reshape.64.nv_ref, ...), custom_call_target="tpu_custom_call" | custom-call | tf_op jit(solution)/shard_map/cross_backward/pallas_call | solution.py:353
  87.4 14.7 %all_to_all.20 = bf16[32,24,128]{2,1,0:T(8,128)(2,1)S(1)} all-to-all(bf16[32,24,128]{2,1,0:T(8,128)(2,1)} %bitcast.38), channel_id=1, replica_groups={{0,1,2,3,4,5,6,7,8,9,10,11,12,13,14,15,16,17,18,19,20,21,22,23,24,25,26..., dimensions={0} | all-to-all | bytes 393216 | tf_op jit(solution)/shard_map/all_to_all | solution.py:444
  102.1 18.7 %all_to_all.21 = bf16[16,24,128]{2,1,0:T(8,128)(2,1)S(1)} all-to-all(bf16[16,24,128]{2,1,0:T(8,128)(2,1)S(1)} %broadcast_in_dim.6), channel_id=1, replica_groups={{0,32,64,96,128,160,192,224,256,288,320,352,384,416,448,480},{4,36,68,1..., dimensions={0} | all-to-all | bytes 196608 | tf_op jit(solution)/shard_map/all_to_all | solution.py:444
  120.9 13.9 %all_to_all.22 = bf16[32,24,128]{2,1,0:T(8,128)(2,1)S(1)} all-to-all(bf16[32,24,128]{2,1,0:T(8,128)(2,1)S(1)} %broadcast_in_dim.7), channel_id=1, replica_groups={{0,1,2,3,4,5,6,7,8,9,10,11,12,13,14,15,16,17,18,19,20,21,22,23,24,25,26..., dimensions={0} | all-to-all | bytes 393216 | tf_op jit(solution)/shard_map/all_to_all | solution.py:444
  134.9 0.1 copy.24
  135.0 0.1 copy.23
  135.1 0.8 copy_bitcast_fusion
  (6 shorter events, 0.2 us)
Async XLA Ops:
  0.6 28.4 %copy-start = (bf16[640,640]{1,0:T(8,128)(2,1)S(1)}, bf16[640,640]{1,0:T(8,128)(2,1)}, u32[]{:S(2)}) copy-start(bf16[640,640]{1,0:T(8,128)(2,1)} %param.35) | copy-start | bytes 2457604
  3.6 38.3 %copy-start.1 = (bf16[640,640]{1,0:T(8,128)(2,1)S(1)}, bf16[640,640]{1,0:T(8,128)(2,1)}, u32[]{:S(2)}) copy-start(bf16[640,640]{1,0:T(8,128)(2,1)} %wq_ref.1) | copy-start | bytes 2457604
  3.6 38.3 %copy-start.3 = (bf16[1,128,640]{2,1,0:T(8,128)(2,1)S(1)}, bf16[1,128,640]{2,1,0:T(8,128)(2,1)}, u32[]{:S(2)}) copy-start(bf16[1,128,640]{2,1,0:T(8,128)(2,1)} %param.18) | copy-start | bytes 491524
  3.6 39.3 %all-to-all-start = ((bf16[128,8,128]{2,1,0:T(8,128)(2,1)}), bf16[128,8,128]{2,1,0:T(8,128)(2,1)S(1)}, u32[]{:S(2)}, u32[]{:S(2)}) async-start(bf16[128,8,128]{2,1,0:T(8,128)(2,1)} %bitcast.32), calls=%async_computation | async-start | bytes 524288 | tf_op jit(solution)/shard_map/all_to_all | solution.py:489
  42.9 0.7 copy-start.2

commit v2 on v1

v2 whole, which is shorter than its diff:
```python
import functools
import math

import jax
import jax.numpy as jnp
from jax import lax
from jax.experimental import pallas as pl
from jax.experimental.pallas import tpu as pltpu
from jax.sharding import PartitionSpec as P

HEAD_DIM = 64
CAP_ROWS = 8
LANES = 128
FEATS = 64

logit_cap = 6.0
norm_eps = 1e-06
score_scale = 1.0 / math.sqrt(HEAD_DIM)

bf16 = jnp.bfloat16
f32 = jnp.float32
i32 = jnp.int32

PLANE = 32
DEPTH = 16
CHUNK = 24
ROW_BLOCK = 256


def iota(shape, dim):
    return lax.broadcasted_iota(i32, shape, dim)


def dot_nn(a, b):
    return lax.dot_general(a, b, (((1,), (0,)), ((), ())), preferred_element_type=f32)


def dot_nt(a, b):
    return lax.dot_general(a, b, (((1,), (1,)), ((), ())), preferred_element_type=f32)


def dot_tn(a, b):
    return lax.dot_general(a, b, (((0,), (0,)), ((), ())), preferred_element_type=f32)


def halves(value):
    high = value.astype(bf16)
    return high, (value - high.astype(f32)).astype(bf16)


def fine_nn(twice, value):
    return dot_nn(twice, jnp.concatenate(halves(value), axis=0))


def fine_tn(a, value):
    both = dot_tn(a, jnp.concatenate(halves(value), axis=1))
    return both[:, : value.shape[1]] + both[:, value.shape[1] :]


def fine_nn_left(value, b):
    high, low = halves(value)
    return dot_nn(high, b) + dot_nn(low, b)


def doubled(hot):
    return jnp.concatenate([hot, hot], axis=1)


def head_sum_matrix(width):
    return jnp.where(
        iota((width, LANES), 0) // HEAD_DIM == iota((width, LANES), 1), 1.0, 0.0
    ).astype(bf16)


def head_spread_matrix(width):
    return jnp.where(
        iota((LANES, width), 1) // HEAD_DIM == iota((LANES, width), 0), 1.0, 0.0
    ).astype(bf16)


def token_hot(x_rows):
    slot = x_rows[:, FEATS : FEATS + 1].astype(f32).astype(i32)
    return jnp.where(iota((x_rows.shape[0], LANES), 1) == slot - 1, 1.0, 0.0).astype(bf16)


def pack_kernel(count_ref, band_ref, slot_ref, inst_ref, raw_ref, out_ref):
    rows = band_ref.shape[1]
    slots = out_ref.shape[0]
    bands = slots // CAP_ROWS
    band = band_ref[...]
    live = iota((1, rows), 1) < count_ref[0]
    dest = jnp.where(live, band, -1)
    named = iota((bands, rows), 0) == dest
    hot = jnp.where(named, 1.0, 0.0).astype(bf16)
    earlier = jnp.where(iota((rows, rows), 0) < iota((rows, rows), 1), 1.0, 0.0).astype(bf16)
    before = dot_nn(hot, earlier)
    rank = jnp.sum(jnp.where(named, before, 0.0), axis=0, keepdims=True).astype(i32)
    position = jnp.where(live, band * CAP_ROWS + rank, -1)
    pick = jnp.where(iota((slots, rows), 0) == position, 1.0, 0.0).astype(bf16)
    part = iota((LANES - FEATS, rows), 0)
    meta = jnp.where(
        part == 0,
        (slot_ref[...] + 1).astype(f32),
        jnp.where(part == 1, inst_ref[...].astype(f32), 0.0),
    ).astype(bf16)
    payload = jnp.concatenate([raw_ref[...], meta], axis=0)
    out_ref[...] = dot_nt(pick, payload).astype(bf16)


def cross_kernel(
    x_ref,
    wk_ref,
    wv_ref,
    table_ref,
    query_ref,
    lines_ref,
    tok_ref,
    cot_ref,
    zq_ref,
    zk_ref,
    zv_ref,
    resid_ref,
    normed_ref,
    key_ref,
    val_ref,
    slope_ref,
    qs_ref,
    tanh_ref,
    prob_ref,
    ntanh_ref,
    nprob_ref,
    lines_out,
    cot_out,
    zq_out,
    zk_out,
    zv_out,
    both_s,
    query_s,
    tok_s,
    hot_s,
    inst_s,
    weight_s,
    sems,
):
    slots = x_ref.shape[0]
    feats, width = wk_ref.shape
    kinds = table_ref.shape[0]
    toks = tok_ref.shape[0]
    first = LANES + kinds
    moves = [
        pltpu.make_async_copy(src, dst, sems.at[k])
        for k, (src, dst) in enumerate(
            (
                (wk_ref, both_s.at[:feats, :width]),
                (wv_ref, both_s.at[:feats, width:]),
                (table_ref, both_s.at[LANES:first, width:]),
                (query_ref, query_s),
                (lines_ref, lines_out),
                (tok_ref, tok_s),
                (zq_ref, zq_out),
                (zk_ref, zk_out),
                (zv_ref, zv_out),
                (cot_ref, cot_out),
            )
        )
    ]
    for move in moves:
        move.start()
    both_s[feats:LANES, :] = jnp.zeros((LANES - feats, 2 * width), bf16)
    both_s[LANES:first, :width] = jnp.zeros((kinds, width), bf16)
    both_s[first:, :] = jnp.zeros((LANES - kinds, 2 * width), bf16)
    head_sum = head_sum_matrix(width)
    head_spread = head_spread_matrix(width)
    for start in range(0, slots, ROW_BLOCK):
        span = pl.ds(start, ROW_BLOCK)
        x = x_ref[span, :]
        hot_s[span, :] = token_hot(x)
        inst = x[:, FEATS + 1 : FEATS + 2].astype(f32).astype(i32)
        inst_s[span, :] = jnp.where(
            iota((ROW_BLOCK, LANES), 1) == inst, 1.0, 0.0
        ).astype(bf16)
    for move in moves[:4]:
        move.wait()
    w_both = both_s[...]
    query = query_s[...]
    total = jnp.zeros((toks, LANES), f32)
    for start in range(0, slots, ROW_BLOCK):
        span = pl.ds(start, ROW_BLOCK)
        hot = hot_s[span, :]
        encoded = dot_nn(jnp.concatenate([x_ref[span, :], inst_s[span, :]], axis=1), w_both)
        keys = encoded[:, :width].astype(bf16)
        key_ref[span, :] = keys
        pre = encoded[:, width:]
        sigma = 1.0 / (1.0 + jnp.exp(-pre))
        val_ref[span, :] = (pre * sigma).astype(bf16)
        slope_ref[span, :] = (sigma * (1.0 + pre * (1.0 - sigma))).astype(bf16)
        q_slot = dot_nn(hot, query).astype(bf16)
        qs_ref[span, :] = q_slot
        t = jnp.tanh(dot_nn(q_slot * keys, head_sum) * (score_scale / logit_cap))
        tanh_ref[span, :] = t
        weight = jnp.exp(logit_cap * t)
        weight_s[span, :] = weight
        total = total + fine_tn(hot, weight)
    for move in moves[4:6]:
        move.wait()
    null_key = lines_out[0:1, :]
    null_val = lines_out[1:2, :]
    gain = lines_out[2:3, :]
    null_t = jnp.tanh(
        fine_nn_left(query.astype(f32) * null_key, head_sum)
        * (score_scale / logit_cap)
    )
    null_weight = jnp.exp(logit_cap * null_t)
    share = 1.0 / (total + null_weight)
    null_prob = null_weight * share
    ntanh_ref[...] = null_t
    nprob_ref[...] = null_prob
    gathered = dot_nn(null_prob.astype(bf16), head_spread) * null_val
    for start in range(0, slots, ROW_BLOCK):
        span = pl.ds(start, ROW_BLOCK)
        hot = hot_s[span, :]
        prob = weight_s[span, :] * fine_nn(doubled(hot), share)
        prob_ref[span, :] = prob
        spread = dot_nn(prob.astype(bf16), head_spread).astype(bf16)
        gathered = gathered + dot_tn(hot, spread * val_ref[span, :])
    resid = (tok_s[...].astype(f32) + gathered).astype(bf16)
    resid_ref[...] = resid
    resid_f = resid.astype(f32)
    inverse = lax.rsqrt(jnp.mean(resid_f * resid_f, axis=1, keepdims=True) + norm_eps)
    normed_ref[...] = (resid_f * inverse * gain).astype(bf16)
    for move in moves[6:]:
        move.wait()


def zonal_kernel(
    me_ref,
    normed_ref,
    att_ref,
    zq_ref,
    zk_ref,
    zv_ref,
    resid_ref,
    cot_ref,
    lines_ref,
    dres_ref,
    zq_s,
    zk_s,
    zkt_s,
    zv_s,
    att_s,
    norm_s,
    dq_s,
    dk_s,
    dv_s,
    top_s,
    prob_s,
    col_s,
):
    whole, width = normed_ref.shape
    own = resid_ref.shape[0]
    sectors = whole // own
    pairs = width // LANES
    me = me_ref[0]
    for k in range(sectors):
        src = pl.multiple_of(lax.rem(me + k, sectors) * own, own)
        norm_s[k * own : (k + 1) * own, :] = normed_ref[pl.ds(src, own), :]
        part = att_ref[pl.ds(src, own), :]
        for p in range(pairs):
            att_s[p, k * own : (k + 1) * own, :] = part[:, p * LANES : (p + 1) * LANES]
    normed = norm_s[...]
    for ref, out in ((zq_ref, zq_s), (zk_ref, zk_s), (zv_ref, zv_s)):
        proj = dot_nn(normed, ref[...])
        for p in range(pairs):
            piece = proj[:, p * LANES : (p + 1) * LANES]
            out[p] = piece.astype(bf16)
            if out is zk_s:
                zkt_s[p] = piece.T.astype(bf16)
    lane_head = iota((whole, LANES), 1) // HEAD_DIM
    low_half = iota((own, LANES), 1) < HEAD_DIM

    def scores(p):
        keys = zk_s[p]
        vals = zv_s[p]
        for head in range(2):
            rows = slice(head * own, (head + 1) * own)
            qm = jnp.where(lane_head == head, zq_s[p], jnp.zeros((), bf16))
            am = jnp.where(lane_head == head, att_s[p], jnp.zeros((), bf16))
            t = jnp.tanh(dot_nt(keys, qm) * (score_scale / logit_cap))
            zdp = dot_nt(vals, am)
            weight = jnp.exp(logit_cap * t)
            share = 1.0 / jnp.sum(weight, axis=0, keepdims=True)
            inner = jnp.sum(weight * zdp, axis=0, keepdims=True) * share
            scaled = share * score_scale
            top = (
                weight[:own] * scaled * (zdp[:own] - inner) * (1.0 - t[:own] * t[:own])
            ).astype(bf16)
            rest = (
                weight[own:, :own]
                * scaled[:, :own]
                * (zdp[own:, :own] - inner[:, :own])
                * (1.0 - t[own:, :own] * t[own:, :own])
            ).astype(bf16)
            top_s[p, rows, :] = top
            prob_s[p, rows, :] = (weight[:own] * share).astype(bf16)
            col_s[p, :own, rows] = top[:, :own]
            col_s[p, own:, rows] = rest

    def gradients(p):
        dk = dot_nn(top_s[p], zq_s[p])
        dk_s[p] = jnp.where(low_half, dk[:own], dk[own:]).astype(bf16)
        dv = dot_nn(prob_s[p], att_s[p])
        dv_s[p] = jnp.where(low_half, dv[:own], dv[own:]).astype(bf16)
        dq = dot_nn(zkt_s[p], col_s[p])
        dq_s[p, :HEAD_DIM, :] = dq[:HEAD_DIM, :own]
        dq_s[p, HEAD_DIM:, :] = dq[HEAD_DIM:, own:]

    for p in range(pairs):
        scores(p)
    for p in range(pairs):
        gradients(p)
    d_normed = jnp.zeros((own, width), f32)
    for p in range(pairs):
        cols = slice(p * LANES, (p + 1) * LANES)
        d_normed = d_normed + dot_nt(dq_s[p].T.astype(bf16), zq_ref[:, cols])
        d_normed = d_normed + dot_nt(dk_s[p], zk_ref[:, cols])
        d_normed = d_normed + dot_nt(dv_s[p], zv_ref[:, cols])
    resid_f = resid_ref[...].astype(f32)
    inverse = lax.rsqrt(jnp.mean(resid_f * resid_f, axis=1, keepdims=True) + norm_eps)
    gained = lines_ref[2:3, :] * d_normed
    dres_ref[...] = (
        cot_ref[...].astype(f32)
        + inverse * gained
        - resid_f * (inverse * inverse * inverse) * jnp.mean(resid_f * gained, axis=1, keepdims=True)
    ).astype(bf16)


def back_kernel(
    x_ref,
    dres_ref,
    lines_ref,
    val_ref,
    slope_ref,
    qs_ref,
    tanh_ref,
    prob_ref,
    ntanh_ref,
    nprob_ref,
    grad_ref,
    draw_ref,
    nraw_ref,
    ds_s,
    dp_s,
    hot_s,
):
    slots = x_ref.shape[0]
    toks, width = dres_ref.shape
    head_sum = head_sum_matrix(width)
    head_spread = head_spread_matrix(width)
    d_resid = dres_ref[...]
    null_prob = nprob_ref[...]
    null_t = ntanh_ref[...]
    null_dp = fine_nn_left(d_resid.astype(f32) * lines_ref[1:2, :], head_sum)
    inner = null_prob * null_dp
    for start in range(0, slots, ROW_BLOCK):
        span = pl.ds(start, ROW_BLOCK)
        hot = token_hot(x_ref[span, :])
        hot_s[span, :] = hot
        d_slot = dot_nn(hot, d_resid).astype(bf16)
        ds_s[span, :] = d_slot
        dp = dot_nn(d_slot * val_ref[span, :], head_sum)
        dp_s[span, :] = dp
        inner = inner + fine_tn(hot, prob_ref[span, :] * dp)
    nraw_ref[...] = null_prob * (null_dp - inner) * (1.0 - null_t * null_t) * score_scale
    grads = jnp.zeros((LANES, 2 * width), f32)
    for start in range(0, slots, ROW_BLOCK):
        span = pl.ds(start, ROW_BLOCK)
        prob = prob_ref[span, :]
        t = tanh_ref[span, :]
        d_raw = (
            prob
            * (dp_s[span, :] - fine_nn(doubled(hot_s[span, :]), inner))
            * (1.0 - t * t)
            * score_scale
        ).astype(bf16)
        draw_ref[span, :] = d_raw
        d_raw_wide = dot_nn(d_raw, head_spread).astype(bf16)
        prob_wide = dot_nn(prob.astype(bf16), head_spread).astype(bf16)
        d_keys = d_raw_wide * qs_ref[span, :]
        d_pre = (prob_wide * ds_s[span, :]) * slope_ref[span, :]
        grads = grads + dot_tn(x_ref[span, :], jnp.concatenate([d_keys, d_pre], axis=1))
    blocks = 2 * width // LANES
    for b in range(blocks):
        grad_ref[b * FEATS : (b + 1) * FEATS, :] = grads[
            :FEATS, b * LANES : (b + 1) * LANES
        ].astype(bf16)
    spare = grad_ref.shape[0] - blocks * FEATS
    grad_ref[blocks * FEATS :, :] = jnp.zeros((spare, LANES), bf16)


def token_kernel(x_ref, dres_ref, lines_ref, key_ref, draw_ref, nraw_ref, wq_ref, dtok_ref):
    slots = x_ref.shape[0]
    head_spread = head_spread_matrix(dres_ref.shape[1])
    d_query = fine_nn_left(nraw_ref[...], head_spread) * lines_ref[0:1, :]
    for start in range(0, slots, ROW_BLOCK):
        span = pl.ds(start, ROW_BLOCK)
        d_raw_wide = dot_nn(draw_ref[span, :], head_spread).astype(bf16)
        hot = token_hot(x_ref[span, :])
        d_query = d_query + dot_tn(hot, d_raw_wide * key_ref[span, :])
    d_tok = dres_ref[...].astype(f32) + dot_nt(d_query.astype(bf16), wq_ref[...])
    dtok_ref[...] = d_tok.astype(bf16)


def in_vmem(value):
    return pltpu.with_memory_space_constraint(value, pltpu.VMEM)


def unpack_kernel(scale, parts_ref, key_ref, value_ref):
    width = key_ref.shape[1]
    pieces = width // LANES
    for g, out in enumerate((key_ref, value_ref)):
        for b in range(pieces):
            start = (g * pieces + b) * FEATS
            rows = parts_ref[start : start + FEATS, :].astype(f32)
            out[:, b * LANES : (b + 1) * LANES] = rows * scale


def in_hbm(value):
    return pltpu.with_memory_space_constraint(value, pltpu.HBM)


def whole_call(
    kernel, name, out_shape, args, scalars=0, fetched=0, far=0, scratch=(), scoped=16
):
    smem = pl.BlockSpec(memory_space=pltpu.SMEM)
    vmem = pl.BlockSpec(memory_space=pltpu.VMEM)
    hbm = pl.BlockSpec(memory_space=pltpu.HBM)
    several = isinstance(out_shape, (list, tuple))
    first, last = scalars + fetched, len(args) - far
    args = (
        tuple(args[:scalars])
        + tuple(in_hbm(a) for a in args[scalars:first])
        + tuple(in_vmem(a) for a in args[first:last])
        + tuple(in_hbm(a) for a in args[last:])
    )
    return pl.pallas_call(
        kernel,
        name=name,
        out_shape=out_shape,
        in_specs=[smem] * scalars + [vmem] * (last - scalars) + [hbm] * far,
        out_specs=[vmem] * len(out_shape) if several else vmem,
        scratch_shapes=list(scratch),
        compiler_params=pltpu.CompilerParams(vmem_limit_bytes=scoped * 1024 * 1024),
    )(*args)


def plain(rows, cols, dtype):
    return jax.ShapeDtypeStruct((rows, cols), dtype)


def shaped(rows, cols, dtype):
    return pltpu.VMEM((rows, cols), dtype)


def pack(obs_count, obs_band, obs_slot, obs_inst, raw_obs, bands):
    rows = raw_obs.shape[0]
    return whole_call(
        pack_kernel,
        "pack",
        plain(bands * CAP_ROWS, LANES, bf16),
        (
            obs_count,
            obs_band.reshape(1, rows),
            obs_slot.reshape(1, rows),
            obs_inst.reshape(1, rows),
            raw_obs.T,
        ),
        scalars=1,
        fetched=4,
    )


def cross_forward(x, w_key, w_val, table, query, lines, tok, cot, zq, zk, zv):
    slots = x.shape[0]
    toks, width = tok.shape
    big = shaped(slots, width, bf16)
    small = shaped(slots, LANES, f32)
    null = shaped(toks, LANES, f32)
    row = shaped(toks, width, bf16)
    square = shaped(*zq.shape, bf16)
    far = (w_key, w_val, table, query, lines, tok, cot, zq, zk, zv)
    return whole_call(
        cross_kernel,
        "cross_forward",
        [row, row, big, big, big, big, small, small, null, null]
        + [shaped(*lines.shape, f32), row, square, square, square],
        (x,) + far,
        far=len(far),
        scratch=(
            pltpu.VMEM((2 * LANES, 2 * width), bf16),
            pltpu.VMEM((toks, width), bf16),
            pltpu.VMEM((toks, width), bf16),
            pltpu.VMEM((slots, LANES), bf16),
            pltpu.VMEM((slots, LANES), bf16),
            pltpu.VMEM((slots, LANES), f32),
            pltpu.SemaphoreType.DMA((len(far),)),
        ),
    )


def zonal(me, normed_all, att_all, zq, zk, zv, resid, cot, lines):
    own, width = resid.shape
    whole = normed_all.shape[0]
    pairs = width // LANES
    rows = pltpu.VMEM((pairs, whole, LANES), bf16)
    return whole_call(
        zonal_kernel,
        "zonal",
        shaped(own, width, bf16),
        (me, normed_all, att_all, zq, zk, zv, resid, cot, lines),
        scalars=1,
        scratch=(
            rows,
            rows,
            pltpu.VMEM((pairs, LANES, whole), bf16),
            rows,
            rows,
            pltpu.VMEM((whole, width), bf16),
            pltpu.VMEM((pairs, LANES, own), f32),
            pltpu.VMEM((pairs, own, LANES), bf16),
            pltpu.VMEM((pairs, own, LANES), bf16),
            pltpu.VMEM((pairs, 2 * own, whole), bf16),
            pltpu.VMEM((pairs, 2 * own, whole), bf16),
            pltpu.VMEM((pairs, whole, 2 * own), bf16),
        ),
    )


def cross_backward(x, d_resid, lines, saved):
    slots = x.shape[0]
    toks, width = d_resid.shape
    return whole_call(
        back_kernel,
        "cross_backward",
        [
            shaped(PLANE * CHUNK, LANES, bf16),
            shaped(slots, LANES, bf16),
            shaped(toks, LANES, f32),
        ],
        (x, d_resid, lines) + tuple(saved),
        scratch=(
            pltpu.VMEM((slots, width), bf16),
            pltpu.VMEM((slots, LANES), f32),
            pltpu.VMEM((slots, LANES), bf16),
        ),
    )


def token_gradient(x, d_resid, lines, keys, d_raw, null_raw, w_query):
    return whole_call(
        token_kernel,
        "token_gradient",
        plain(*d_resid.shape, bf16),
        (x, d_resid, lines, keys, d_raw, null_raw, w_query),
    )


def unpack(parts, width, scale):
    out = plain(FEATS, width, f32)
    return whole_call(
        functools.partial(unpack_kernel, scale), "unpack", [out, out], (parts,)
    )


def sum_everywhere(rows):
    plane = [list(range(z * PLANE, (z + 1) * PLANE)) for z in range(DEPTH)]
    lats = PLANE // 4
    column = [[z * lats + k for z in range(DEPTH)] for k in range(lats)]

    def swap(parts, axes, groups):
        return lax.all_to_all(
            parts, axes, split_axis=0, concat_axis=0, tiled=True, axis_index_groups=groups
        )

    def total(parts):
        return jnp.sum(parts.astype(f32), axis=0)

    parts = swap(rows.reshape(PLANE, CHUNK, LANES), ("lat", "lon"), plane)
    mine = total(parts).astype(bf16)
    parts = swap(jnp.broadcast_to(mine, (DEPTH, CHUNK, LANES)), "lat", column)
    mine = total(parts).astype(bf16)
    parts = swap(jnp.broadcast_to(mine, (PLANE, CHUNK, LANES)), ("lat", "lon"), plane)
    return parts.reshape(PLANE * CHUNK, LANES)


def on_device(
    tokens,
    cotangent,
    raw_obs,
    obs_band,
    obs_slot,
    obs_inst,
    obs_count,
    w_key_obs,
    w_val_obs,
    inst_table,
    null_key,
    null_val,
    w_query,
    norm_gain,
    zonal_query,
    zonal_key,
    zonal_value,
    zonal_out,
):
    tok_rows, width = tokens.shape[1:]
    bands = lax.axis_size("lat")
    devices = bands * lax.axis_size("lon")
    obs_total = raw_obs.shape[0] * devices
    tok = tokens.reshape(tok_rows, width)
    cot = cotangent.reshape(tok_rows, width)
    lines = jnp.stack([null_key.astype(f32), null_val.astype(f32), norm_gain])
    lines = jnp.concatenate([lines, jnp.zeros((5, width), f32)], axis=0)
    packed = pack(obs_count, obs_band, obs_slot, obs_inst, raw_obs, bands)
    received = lax.all_to_all(
        packed.reshape(bands, CAP_ROWS, LANES), "lat", split_axis=0, concat_axis=0, tiled=True
    ).reshape(bands * CAP_ROWS, LANES)
    query = jnp.dot(tok, w_query, preferred_element_type=f32).astype(bf16)
    d_att = dot_nt(cot, zonal_out).astype(bf16)
    att_all = lax.all_gather(d_att, "lon", axis=0, tiled=True)
    resid, normed, keys, *saved, lines, cot, zq, zk, zv = cross_forward(
        received,
        w_key_obs,
        w_val_obs,
        inst_table,
        query,
        lines,
        tok,
        cot,
        zonal_query,
        zonal_key,
        zonal_value,
    )
    normed_all = lax.all_gather(normed, "lon", axis=0, tiled=True)
    me = lax.axis_index("lon").astype(i32).reshape(1)
    d_resid = zonal(me, normed_all, att_all, zq, zk, zv, resid, cot, lines)
    grads, d_raw, null_raw = cross_backward(received, d_resid, lines, saved)
    d_tok = token_gradient(received, d_resid, lines, keys, d_raw, null_raw, w_query)
    key_grad, value_grad = unpack(sum_everywhere(grads), width, 1.0 / math.sqrt(obs_total))
    return d_tok.reshape(1, tok_rows, width), key_grad, value_grad


def solution(mesh):
    return jax.shard_map(
        on_device,
        mesh=mesh,
        in_specs=(
            P("lat", "lon", None),
            P("lat", "lon", None),
            P(("lat", "lon"), None),
            P(("lat", "lon"), None),
            P(("lat", "lon")),
            P(("lat", "lon")),
            P(("lat", "lon")),
            P(),
            P(),
            P(),
            P(),
            P(),
            P(),
            P(),
            P(),
            P(),
            P(),
            P(),
        ),
        out_specs=(P("lat", "lon", None), P(), P()),
        check_vma=False,
    )
```

time: 136 us -> 124 us (0.912)
  blocking collectives: 72.5 us -> 56.7 us
  Pallas kernels: 32.4 us -> 23.6 us
  starting transfers between devices: 21.6 us -> 27.8 us
  waiting for transfers between devices: 0.01 us -> 5.55 us
    all_to_all x3 -> x2, blocking collectives: 47.3 us -> 32 us  [swap(): lax.all_to_all(parts, axes, split_axis=0, concat_axis=0, tiled=True, axis...]
    pallas_call x4 -> x6, Pallas kernels: 32.4 us -> 23.6 us  [whole_call(): pl.pallas_call(kernel, name=name, out_shape=out_shape, in_specs=[smem] *...]
    all_to_all x0 -> x1, starting transfers between devices: none -> 6.2 us  [swap(): lax.all_to_all(parts, axes, split_axis=0, concat_axis=0, tiled=True, axis...]
    all_to_all x0 -> x1, waiting for transfers between devices: none -> 4.71 us  [swap(): lax.all_to_all(parts, axes, split_axis=0, concat_axis=0, tiled=True, axis...]
    reshape x3 -> x0, local copies, waits for them, and re-layouts: 3.81 us -> none  [the longest x1 1.28 us: on_device(): null_key = null_key.reshape(1, width)]
    another operation x0 -> x3, local copies, waits for them, and re-layouts: none -> 2.06 us  [on_device(): lines = jnp.stack([null_key.astype(f32), null_val.astype(f32), norm_gain])]
    unnamed x8 -> x10, local copies, waits for them, and re-layouts: 0.72 us -> 2.4 us
  transfers between devices with their start and end apart: 1 -> 2, of which waited for: 0 -> 2; matrix products, arithmetic and copies ran while one was open for 4% -> 4% of each run, Pallas kernels for 0% -> 2%
where the time goes in v2:
time: 124 us; the launch traced here: 123 us
  blocking collectives  56.7 us (46%)
  starting transfers between devices  27.8 us (22%)
  Pallas kernels  23.6 us (19%)
  waiting for transfers between devices  5.55 us (4%)
  local copies, waits for them, and re-layouts  5.26 us (4%)
  matrix products  2.26 us (2%)
  between operations  1.45 us (1%)
    all_to_all x2, blocking collectives, swap(): lax.all_to_all(parts, axes, split_axis=0, concat_axis=0, tiled=True, axis...  32 us
    pallas_call x6, Pallas kernels, whole_call(): pl.pallas_call(kernel, name=name, out_shape=out_shape, in_specs=[smem] *...  23.6 us
    all_to_all x1, starting transfers between devices, on_device(): lax.all_to_all(packed.reshape(bands, CAP_ROWS, LANES), 'lat', split_axis=...  21.6 us
    all_gather x1, blocking collectives, on_device(): normed_all = lax.all_gather(normed, 'lon', axis=0, tiled=True)  13.5 us
    all_gather x1, blocking collectives, on_device(): att_all = lax.all_gather(d_att, 'lon', axis=0, tiled=True)  11.1 us
    all_to_all x1, starting transfers between devices, swap(): lax.all_to_all(parts, axes, split_axis=0, concat_axis=0, tiled=True, axis...  6.2 us
    all_to_all x1, waiting for transfers between devices, swap(): lax.all_to_all(parts, axes, split_axis=0, concat_axis=0, tiled=True, axis...  4.71 us
  transfers between devices with their start and end apart: 2, of which 2 were waited for; matrix products, arithmetic and copies ran while one was open for 4% of the time, Pallas kernels for 2%

profile of v2, /device:TPU:1, one launch (start us, length us, event | category | flops | bytes accessed | tf_op | source)
XLA Modules:
  0.0 123.3 jit_solution(12273129839428494060)
XLA Ops:
  0.6 0.0 copy-start
  1.4 2.3 %pack.1 = bf16[1024,128]{1,0:T(8,128)(2,1)} custom-call(s32[1]{0:T(128)S(6)} %copy.21.count_ref, s32[1,512]{1,0:T(1,128)} %bitcast.27, s32[1,512]{1,0:T(1,128)} %bitcast.28, s32[1,512]{1,0:T(1,128)} %bitcast.29, bf16[64,512]{1,0:T(8,128)(2,1)} %bitcast.26), custom_call_target="tpu_custom_call" | custom-call | tf_op jit(solution)/shard_map/pack/pallas_call | solution.py:445
  3.6 0.0 copy-start.1
  3.6 0.0 copy-start.4
  3.6 21.6 %all-to-all-start = ((bf16[128,8,128]{2,1,0:T(8,128)(2,1)}), bf16[128,8,128]{2,1,0:T(8,128)(2,1)S(1)}, u32[]{:S(2)}, u32[]{:S(2)}) async-start(bf16[128,8,128]{2,1,0:T(8,128)(2,1)} %bitcast.4), calls=%async_computation | async-start | bytes 524288 | tf_op jit(solution)/shard_map/all_to_all | solution.py:624
  25.2 0.7 reshape.50
  25.9 0.7 reshape.51
  26.6 0.7 stack.19
  27.3 0.1 pad.3.clone
  27.3 0.7 maximum_maximum_fusion.lines_ref
  28.0 0.0 copy-done
  28.0 1.3 %convolution_convert_fusion = bf16[128,640]{1,0:T(8,128)(2,1)S(1)} fusion(bf16[640,640]{1,0:T(8,128)(2,1)S(1)} %copy-done, bf16[1,128,640]{2,1,0:T(8,128)(2,1)} %param.19), kind=kOutput, calls=%fused_computation | convolution fusion | flops 104939520 | bytes 1146880 | tf_op jit(solution)/shard_map/dot_general | solution.py:39
  29.3 11.1 %all_gather.7.att_ref = bf16[512,640]{1,0:T(8,128)(2,1)S(1)} all-gather(bf16[128,640]{1,0:T(8,128)(2,1)S(1)} %convolution_convert_fusion), channel_id=1, replica_groups=mesh['lat'=128,'lon'=4] {'lon'}, dimensions={0}, use_global_device_ids=true | all-gather | bytes 819200 | tf_op jit(solution)/shard_map/all_gather | solution.py:629
  40.5 0.0 copy-done.1
  40.5 0.0 copy-done.4
  40.5 1.0 convolution_convert_fusion.1.query_ref
  41.4 0.8 all-to-all-done
  42.3 5.9 %cross_forward.1 = (bf16[128,640]{1,0:T(8,128)(2,1)S(1)}, bf16[128,640]{1,0:T(8,128)(2,1)S(1)}, bf16[1024,640]{1,0:T(8,128)(2,1)S(1)}, bf16[1024,640]{1,0:T(8,12...) custom-call(bf16[1024,128]{1,0:T(8,128)(2,1)S(1)} %bitcast.18, ...), custom_call_target="tpu_custom_call" | custom-call | tf_op jit(solution)/shard_map/cross_forward/pallas_call | solution.py:445
  48.2 0.0 copy-start.2
  48.2 1.1 copy-done.2
  49.2 13.5 %all_gather.6.normed_ref = bf16[512,640]{1,0:T(8,128)(2,1)S(1)} all-gather(bf16[128,640]{1,0:T(8,128)(2,1)S(1)} %get-tuple-element.23), channel_id=1, replica_groups=mesh['lat'=128,'lon'=4] {'lon'}, dimensions={0}, use_global_device_ids=true | all-gather | bytes 819200 | tf_op jit(solution)/shard_map/all_gather | solution.py:643
  62.8 8.8 %zonal.1.dres_ref = bf16[128,640]{1,0:T(8,128)(2,1)S(1)} custom-call(s32[1]{0:T(128)} %bitcast.6.me_ref, bf16[512,640]{1,0:T(8,128)(2,1)S(1)} %all_gather.6.normed_ref, bf16[512,640]{1,0:T(8,128)(2,1)S(1)} %all_gather.7.att_ref, bf16[640,640]{1,0:T(8,128)(2,1)S(1)} %get-tuple-element.24.zq_ref, bf16[640,640]{1,0:T(8,128)(2,1)S(1)} %get-tuple-element.25.zk_ref, ...), custom_call_target="tpu_custom_call" | custom-call | tf_op jit(solution)/shard_map/zonal/pallas_call | solution.py:445
  71.6 3.8 %cross_backward.1 = (bf16[768,128]{1,0:T(8,128)(2,1)S(1)}, bf16[1024,128]{1,0:T(8,128)(2,1)S(1)}, f32[128,128]{1,0:T(8,128)S(1)}) custom-call(bf16[1024,128]{1,0:T(8,128)(2,1)S(1)} %bitcast.19, bf16[128,640]{1,0:T(8,128)(2,1)S(1)} %zonal.1.dres_ref, f32[8,640]{1,0:T(8,128)S(1)} %get-tuple-element.29.lines_ref, ...), custom_call_target="tpu_custom_call" | custom-call | tf_op jit(solution)/shard_map/cross_backward/pallas_call | solution.py:445
  75.3 14.6 %all_to_all.20 = bf16[32,24,128]{2,1,0:T(8,128)(2,1)S(1)} all-to-all(bf16[32,24,128]{2,1,0:T(8,128)(2,1)S(1)} %bitcast.22), channel_id=1, replica_groups={{0,1,2,3,4,5,6,7,8,9,10,11,12,13,14,15,16,17,18,19,20,21,22,23,24,25,26..., dimensions={0} | all-to-all | bytes 393216 | tf_op jit(solution)/shard_map/all_to_all | solution.py:580
  90.0 17.5 %all_to_all.21 = bf16[16,24,128]{2,1,0:T(8,128)(2,1)S(1)} all-to-all(bf16[16,24,128]{2,1,0:T(8,128)(2,1)S(1)} %broadcast_in_dim.10), channel_id=1, replica_groups={{0,32,64,96,128,160,192,224,256,288,320,352,384,416,448,480},{4,36,68,1..., dimensions={0} | all-to-all | bytes 196608 | tf_op jit(solution)/shard_map/all_to_all | solution.py:580
  107.5 0.7 broadcast_in_dim.11
  108.2 6.2 %all-to-all-start.3 = ((bf16[32,24,128]{2,1,0:T(8,128)(2,1)}), bf16[32,24,128]{2,1,0:T(8,128)(2,1)S(1)}, u32[]{:S(2)}, u32[]{:S(2)}) async-start(bf16[32,24,128]{2,1,0:T(8,128)(2,1)} %broadcast_in_dim.11), calls=%async_computation.3 | async-start | bytes 393216 | tf_op jit(solution)/shard_map/all_to_all | solution.py:580
  114.4 0.0 copy-start.3
  114.4 1.3 %copy-done.3 = bf16[1024,640]{1,0:T(8,128)(2,1)S(1)} copy-done((bf16[1024,640]{1,0:T(8,128)(2,1)S(1)}, bf16[1024,640]{1,0:T(8,128)(2,1)}, u32[]{:S(2)}) %copy-start.3) | copy-done | bytes 1310744
  115.7 2.2 %token_gradient.1 = bf16[128,640]{1,0:T(8,128)(2,1)} custom-call(bf16[1024,128]{1,0:T(8,128)(2,1)S(1)} %bitcast.20, bf16[128,640]{1,0:T(8,128)(2,1)S(1)} %zonal.1.dres_ref, f32[8,640]{1,0:T(8,128)S(1)} %get-tuple-element.29.lines_ref, bf16[1024,640]{1,0:T(8,128)(2,1)S(1)} %copy-done.3, bf16[1024,128]{1,0:T(8,128)(2,1)S(1)} %get-tuple-element.38.draw_ref, ...), custom_call_target="tpu_custom_call" | custom-call | tf_op jit(solution)/shard_map/token_gradient/pallas_call | solution.py:445
  117.9 4.7 %all-to-all-done.3 = bf16[32,24,128]{2,1,0:T(8,128)(2,1)S(1)} async-done(((bf16[32,24,128]{2,1,0:T(8,128)(2,1)}), bf16[32,24,128]{2,1,0:T(8,128)(2,1)S(1)}, u32[]{:S(2)}, u32[]{:S(2)}) %all-to-all-start.3) | async-done | bytes 196640 | tf_op jit(solution)/shard_map/all_to_all | solution.py:580
  122.6 0.7 unpack.1
  (4 shorter events, 0.1 us)
Async XLA Ops:
  0.6 27.4 %copy-start = (bf16[640,640]{1,0:T(8,128)(2,1)S(1)}, bf16[640,640]{1,0:T(8,128)(2,1)}, u32[]{:S(2)}) copy-start(bf16[640,640]{1,0:T(8,128)(2,1)} %param.35) | copy-start | bytes 2457604
  3.6 36.8 %copy-start.1 = (bf16[640,640]{1,0:T(8,128)(2,1)S(1)}, bf16[640,640]{1,0:T(8,128)(2,1)}, u32[]{:S(2)}) copy-start(bf16[640,640]{1,0:T(8,128)(2,1)} %wq_ref.1) | copy-start | bytes 2457604
  3.6 36.8 %copy-start.4 = (bf16[1,128,640]{2,1,0:T(8,128)(2,1)S(1)}, bf16[1,128,640]{2,1,0:T(8,128)(2,1)}, u32[]{:S(2)}) copy-start(bf16[1,128,640]{2,1,0:T(8,128)(2,1)} %param.18) | copy-start | bytes 491524
  3.6 38.7 %all-to-all-start = ((bf16[128,8,128]{2,1,0:T(8,128)(2,1)}), bf16[128,8,128]{2,1,0:T(8,128)(2,1)S(1)}, u32[]{:S(2)}, u32[]{:S(2)}) async-start(bf16[128,8,128]{2,1,0:T(8,128)(2,1)} %bitcast.4), calls=%async_computation | async-start | bytes 524288 | tf_op jit(solution)/shard_map/all_to_all | solution.py:624
  48.2 1.1 copy-start.2
  108.2 14.4 %all-to-all-start.3 = ((bf16[32,24,128]{2,1,0:T(8,128)(2,1)}), bf16[32,24,128]{2,1,0:T(8,128)(2,1)S(1)}, u32[]{:S(2)}, u32[]{:S(2)}) async-start(bf16[32,24,128]{2,1,0:T(8,128)(2,1)} %broadcast_in_dim.11), calls=%async_computation.3 | async-start | bytes 393216 | tf_op jit(solution)/shard_map/all_to_all | solution.py:580
  114.4 1.3 %copy-start.3 = (bf16[1024,640]{1,0:T(8,128)(2,1)S(1)}, bf16[1024,640]{1,0:T(8,128)(2,1)}, u32[]{:S(2)}) copy-start(bf16[1024,640]{1,0:T(8,128)(2,1)} %copy-done.2) | copy-start | bytes 3932164

commit v3 on v2

--- a/solution.py
+++ b/solution.py
@@ -16,6 +16,7 @@
 logit_cap = 6.0
 norm_eps = 1e-06
 score_scale = 1.0 / math.sqrt(HEAD_DIM)
+LOG2E = math.log2(math.e)
 
 bf16 = jnp.bfloat16
 f32 = jnp.float32
@@ -24,7 +25,7 @@
 PLANE = 32
 DEPTH = 16
 CHUNK = 24
-ROW_BLOCK = 256
+ROW_BLOCK = 1024
 
 
 def iota(shape, dim):
@@ -83,20 +84,49 @@
     return jnp.where(iota((x_rows.shape[0], LANES), 1) == slot - 1, 1.0, 0.0).astype(bf16)
 
 
-def pack_kernel(count_ref, band_ref, slot_ref, inst_ref, raw_ref, out_ref):
+def pack_kernel(
+    count_ref,
+    band_hbm,
+    slot_hbm,
+    inst_hbm,
+    raw_hbm,
+    out_hbm,
+    band_ref,
+    slot_ref,
+    inst_ref,
+    raw_ref,
+    out_ref,
+    in_sems,
+    out_sems,
+):
+    moves = [
+        pltpu.make_async_copy(src, dst, in_sems.at[k])
+        for k, (src, dst) in enumerate(
+            (
+                (band_hbm, band_ref),
+                (raw_hbm, raw_ref),
+                (slot_hbm, slot_ref),
+                (inst_hbm, inst_ref),
+            )
+        )
+    ]
+    for move in moves:
+        move.start()
     rows = band_ref.shape[1]
     slots = out_ref.shape[0]
     bands = slots // CAP_ROWS
+    earlier = jnp.where(iota((rows, rows), 0) < iota((rows, rows), 1), 1.0, 0.0).astype(bf16)
+    moves[0].wait()
     band = band_ref[...]
     live = iota((1, rows), 1) < count_ref[0]
     dest = jnp.where(live, band, -1)
     named = iota((bands, rows), 0) == dest
     hot = jnp.where(named, 1.0, 0.0).astype(bf16)
-    earlier = jnp.where(iota((rows, rows), 0) < iota((rows, rows), 1), 1.0, 0.0).astype(bf16)
     before = dot_nn(hot, earlier)
     rank = jnp.sum(jnp.where(named, before, 0.0), axis=0, keepdims=True).astype(i32)
     position = jnp.where(live, band * CAP_ROWS + rank, -1)
-    pick = jnp.where(iota((slots, rows), 0) == position, 1.0, 0.0).astype(bf16)
+    for move in moves[1:]:
+        move.wait()
     part = iota((LANES - FEATS, rows), 0)
     meta = jnp.where(
         part == 0,
@@ -104,7 +134,18 @@
         jnp.where(part == 1, inst_ref[...].astype(f32), 0.0),
     ).astype(bf16)
     payload = jnp.concatenate([raw_ref[...], meta], axis=0)
-    out_ref[...] = dot_nt(pick, payload).astype(bf16)
+    step = slots // out_sems.shape[0]
+    leaving = []
+    for k in range(out_sems.shape[0]):
+        span = pl.ds(k * step, step)
+        pick = jnp.where(iota((step, rows), 0) + k * step == position, 1.0, 0.0).astype(bf16)
+        out_ref[span, :] = dot_nt(pick, payload).astype(bf16)
+        leaving.append(
+            pltpu.make_async_copy(out_ref.at[span], out_hbm.at[span], out_sems.at[k])
+        )
+        leaving[-1].start()
+    for move in leaving:
+        move.wait()
 
 
 def cross_kernel(
@@ -137,10 +178,12 @@
     both_s,
     query_s,
     tok_s,
+    keys_s,
     hot_s,
     inst_s,
     weight_s,
     sems,
+    key_sem,
 ):
     slots = x_ref.shape[0]
     feats, width = wk_ref.shape
@@ -164,7 +207,7 @@
             )
         )
     ]
-    for move in moves:
+    for move in moves[:6]:
         move.start()
     both_s[feats:LANES, :] = jnp.zeros((LANES - feats, 2 * width), bf16)
     both_s[LANES:first, :width] = jnp.zeros((kinds, width), bf16)
@@ -181,6 +224,8 @@
         ).astype(bf16)
     for move in moves[:4]:
         move.wait()
+    for move in moves[6:]:
+        move.start()
     w_both = both_s[...]
     query = query_s[...]
     total = jnp.zeros((toks, LANES), f32)
@@ -189,9 +234,9 @@
         hot = hot_s[span, :]
         encoded = dot_nn(jnp.concatenate([x_ref[span, :], inst_s[span, :]], axis=1), w_both)
         keys = encoded[:, :width].astype(bf16)
-        key_ref[span, :] = keys
+        keys_s[span, :] = keys
         pre = encoded[:, width:]
-        sigma = 1.0 / (1.0 + jnp.exp(-pre))
+        sigma = 0.5 + 0.5 * jnp.tanh(0.5 * pre)
         val_ref[span, :] = (pre * sigma).astype(bf16)
         slope_ref[span, :] = (sigma * (1.0 + pre * (1.0 - sigma))).astype(bf16)
         q_slot = dot_nn(hot, query).astype(bf16)
@@ -201,6 +246,8 @@
         weight = jnp.exp(logit_cap * t)
         weight_s[span, :] = weight
         total = total + fine_tn(hot, weight)
+    away = pltpu.make_async_copy(keys_s, key_ref, key_sem)
+    away.start()
     for move in moves[4:6]:
         move.wait()
     null_key = lines_out[0:1, :]
@@ -230,6 +277,7 @@
     normed_ref[...] = (resid_f * inverse * gain).astype(bf16)
     for move in moves[6:]:
         move.wait()
+    away.wait()
 
 
 def zonal_kernel(
@@ -274,7 +322,7 @@
             piece = proj[:, p * LANES : (p + 1) * LANES]
             out[p] = piece.astype(bf16)
             if out is zk_s:
-                zkt_s[p] = piece.T.astype(bf16)
+                zkt_s[p] = piece.astype(bf16).T
     lane_head = iota((whole, LANES), 1) // HEAD_DIM
     low_half = iota((own, LANES), 1) < HEAD_DIM
 
@@ -285,45 +333,48 @@
             rows = slice(head * own, (head + 1) * own)
             qm = jnp.where(lane_head == head, zq_s[p], jnp.zeros((), bf16))
             am = jnp.where(lane_head == head, att_s[p], jnp.zeros((), bf16))
-            t = jnp.tanh(dot_nt(keys, qm) * (score_scale / logit_cap))
-            zdp = dot_nt(vals, am)
-            weight = jnp.exp(logit_cap * t)
-            share = 1.0 / jnp.sum(weight, axis=0, keepdims=True)
-            inner = jnp.sum(weight * zdp, axis=0, keepdims=True) * share
-            scaled = share * score_scale
-            top = (
-                weight[:own] * scaled * (zdp[:own] - inner) * (1.0 - t[:own] * t[:own])
-            ).astype(bf16)
-            rest = (
-                weight[own:, :own]
-                * scaled[:, :own]
-                * (zdp[own:, :own] - inner[:, :own])
-                * (1.0 - t[own:, :own] * t[own:, :own])
-            ).astype(bf16)
-            top_s[p, rows, :] = top
-            prob_s[p, rows, :] = (weight[:own] * share).astype(bf16)
-            col_s[p, :own, rows] = top[:, :own]
-            col_s[p, own:, rows] = rest
+            half = whole // 2
+            for start in (0, half):
+                cols = slice(start, start + half)
+                t = jnp.tanh(dot_nt(keys, qm[cols]) * (score_scale / logit_cap))
+                zdp = dot_nt(vals, am[cols])
+                weight = jnp.exp2((logit_cap * LOG2E) * t)
+                share = 1.0 / jnp.sum(weight, axis=0, keepdims=True)
+                inner = jnp.sum(weight * zdp, axis=0, keepdims=True) * share
+                t_top = t[:own]
+                prob = weight[:own] * share
+                top = (prob * (zdp[:own] - inner) * (1.0 - t_top * t_top)).astype(bf16)
+                top_s[p, rows, cols] = top
+                prob_s[p, rows, cols] = prob.astype(bf16)
+                if start == 0:
+                    t_rest = t[own:, :own]
+                    rest = (
+                        (weight[own:, :own] * share[:, :own])
+                        * (zdp[own:, :own] - inner[:, :own])
+                        * (1.0 - t_rest * t_rest)
+                    ).astype(bf16)
+                    col_s[p, :own, rows] = top[:, :own]
+                    col_s[p, own:, rows] = rest
 
     def gradients(p):
         dk = dot_nn(top_s[p], zq_s[p])
-        dk_s[p] = jnp.where(low_half, dk[:own], dk[own:]).astype(bf16)
+        dk_s[p] = (jnp.where(low_half, dk[:own], dk[own:]) * score_scale).astype(bf16)
         dv = dot_nn(prob_s[p], att_s[p])
         dv_s[p] = jnp.where(low_half, dv[:own], dv[own:]).astype(bf16)
         dq = dot_nn(zkt_s[p], col_s[p])
-        dq_s[p, :HEAD_DIM, :] = dq[:HEAD_DIM, :own]
-        dq_s[p, HEAD_DIM:, :] = dq[HEAD_DIM:, own:]
+        dq_s[p, :HEAD_DIM, :] = dq[:HEAD_DIM, :own] * score_scale
+        dq_s[p, HEAD_DIM:, :] = dq[HEAD_DIM:, own:] * score_scale
 
     for p in range(pairs):
         scores(p)
     for p in range(pairs):
         gradients(p)
-    d_normed = jnp.zeros((own, width), f32)
-    for p in range(pairs):
-        cols = slice(p * LANES, (p + 1) * LANES)
-        d_normed = d_normed + dot_nt(dq_s[p].T.astype(bf16), zq_ref[:, cols])
-        d_normed = d_normed + dot_nt(dk_s[p], zk_ref[:, cols])
-        d_normed = d_normed + dot_nt(dv_s[p], zv_ref[:, cols])
+    d_zq = jnp.concatenate([dq_s[p].T.astype(bf16) for p in range(pairs)], axis=1)
+    d_zk = jnp.concatenate([dk_s[p] for p in range(pairs)], axis=1)
+    d_zv = jnp.concatenate([dv_s[p] for p in range(pairs)], axis=1)
+    d_normed = (
+        dot_nt(d_zq, zq_ref[...]) + dot_nt(d_zk, zk_ref[...]) + dot_nt(d_zv, zv_ref[...])
+    )
     resid_f = resid_ref[...].astype(f32)
     inverse = lax.rsqrt(jnp.mean(resid_f * resid_f, axis=1, keepdims=True) + norm_eps)
     gained = lines_ref[2:3, :] * d_normed
@@ -397,16 +448,34 @@
     grad_ref[blocks * FEATS :, :] = jnp.zeros((spare, LANES), bf16)
 
 
-def token_kernel(x_ref, dres_ref, lines_ref, key_ref, draw_ref, nraw_ref, wq_ref, dtok_ref):
+def token_kernel(
+    x_ref,
+    dres_ref,
+    lines_ref,
+    draw_ref,
+    nraw_ref,
+    key_ref,
+    wq_ref,
+    dtok_ref,
+    keys_s,
+    wq_s,
+    sems,
+):
     slots = x_ref.shape[0]
+    keys_move = pltpu.make_async_copy(key_ref, keys_s, sems.at[0])
+    wq_move = pltpu.make_async_copy(wq_ref, wq_s, sems.at[1])
+    keys_move.start()
+    wq_move.start()
     head_spread = head_spread_matrix(dres_ref.shape[1])
     d_query = fine_nn_left(nraw_ref[...], head_spread) * lines_ref[0:1, :]
+    keys_move.wait()
     for start in range(0, slots, ROW_BLOCK):
         span = pl.ds(start, ROW_BLOCK)
         d_raw_wide = dot_nn(draw_ref[span, :], head_spread).astype(bf16)
         hot = token_hot(x_ref[span, :])
-        d_query = d_query + dot_tn(hot, d_raw_wide * key_ref[span, :])
-    d_tok = dres_ref[...].astype(f32) + dot_nt(d_query.astype(bf16), wq_ref[...])
+        d_query = d_query + dot_tn(hot, d_raw_wide * keys_s[span, :])
+    wq_move.wait()
+    d_tok = dres_ref[...].astype(f32) + dot_nt(d_query.astype(bf16), wq_s[...])
     dtok_ref[...] = d_tok.astype(bf16)
 
 
@@ -429,7 +498,7 @@
 
 
 def whole_call(
-    kernel, name, out_shape, args, scalars=0, fetched=0, far=0, scratch=(), scoped=16
+    kernel, name, out_shape, args, scalars=0, fetched=0, far=0, away=(), scratch=(), scoped=16
 ):
     smem = pl.BlockSpec(memory_space=pltpu.SMEM)
     vmem = pl.BlockSpec(memory_space=pltpu.VMEM)
@@ -447,7 +516,9 @@
         name=name,
         out_shape=out_shape,
         in_specs=[smem] * scalars + [vmem] * (last - scalars) + [hbm] * far,
-        out_specs=[vmem] * len(out_shape) if several else vmem,
+        out_specs=[hbm if k in away else vmem for k in range(len(out_shape))]
+        if several
+        else vmem,
         scratch_shapes=list(scratch),
         compiler_params=pltpu.CompilerParams(vmem_limit_bytes=scoped * 1024 * 1024),
     )(*args)
@@ -462,11 +533,13 @@
 
 
 def pack(obs_count, obs_band, obs_slot, obs_inst, raw_obs, bands):
-    rows = raw_obs.shape[0]
+    rows, feats = raw_obs.shape
+    slots = bands * CAP_ROWS
+    line = pltpu.VMEM((1, rows), i32)
     return whole_call(
         pack_kernel,
         "pack",
-        plain(bands * CAP_ROWS, LANES, bf16),
+        [plain(slots, LANES, bf16)],
         (
             obs_count,
             obs_band.reshape(1, rows),
@@ -475,8 +548,18 @@
             raw_obs.T,
         ),
         scalars=1,
-        fetched=4,
-    )
+        far=4,
+        away=(0,),
+        scratch=(
+            line,
+            line,
+            line,
+            pltpu.VMEM((feats, rows), bf16),
+            pltpu.VMEM((slots, LANES), bf16),
+            pltpu.SemaphoreType.DMA((4,)),
+            pltpu.SemaphoreType.DMA((4,)),
+        ),
+    )[0]
 
 
 def cross_forward(x, w_key, w_val, table, query, lines, tok, cot, zq, zk, zv):
@@ -491,18 +574,21 @@
     return whole_call(
         cross_kernel,
         "cross_forward",
-        [row, row, big, big, big, big, small, small, null, null]
+        [row, row, pltpu.HBM((slots, width), bf16), big, big, big, small, small, null, null]
         + [shaped(*lines.shape, f32), row, square, square, square],
         (x,) + far,
         far=len(far),
+        away=(2,),
         scratch=(
             pltpu.VMEM((2 * LANES, 2 * width), bf16),
             pltpu.VMEM((toks, width), bf16),
             pltpu.VMEM((toks, width), bf16),
+            pltpu.VMEM((slots, width), bf16),
             pltpu.VMEM((slots, LANES), bf16),
             pltpu.VMEM((slots, LANES), bf16),
             pltpu.VMEM((slots, LANES), f32),
             pltpu.SemaphoreType.DMA((len(far),)),
+            pltpu.SemaphoreType.DMA(()),
         ),
     )
 
@@ -560,7 +646,13 @@
         token_kernel,
         "token_gradient",
         plain(*d_resid.shape, bf16),
-        (x, d_resid, lines, keys, d_raw, null_raw, w_query),
+        (x, d_resid, lines, d_raw, null_raw, keys, w_query),
+        far=2,
+        scratch=(
+            pltpu.VMEM(keys.shape, bf16),
+            pltpu.VMEM(w_query.shape, bf16),
+            pltpu.SemaphoreType.DMA((2,)),
+        ),
     )
 
 

time: 124 us -> 120 us (0.968)
  local copies, waits for them, and re-layouts: 5.26 us -> 2.9 us
  Pallas kernels: 23.6 us -> 21.8 us
    unnamed x10 -> x6, local copies, waits for them, and re-layouts: 2.4 us -> 0.02 us
    pallas_call x6, Pallas kernels: 23.6 us -> 21.8 us  [whole_call(): pl.pallas_call(kernel, name=name, out_shape=out_shape, in_specs=[smem] *...]
  transfers between devices with their start and end apart: 2 -> 2, of which waited for: 2 -> 2; matrix products, arithmetic and copies ran while one was open for 4% -> 4% of each run, Pallas kernels for 2% -> 3%
where the time goes in v3:
time: 120 us
  blocking collectives  56.7 us (47%)
  starting transfers between devices  27.8 us (23%)
  Pallas kernels  21.8 us (18%)
  waiting for transfers between devices  5.9 us (5%)
  local copies, waits for them, and re-layouts  2.9 us (2%)
  matrix products  2.26 us (2%)
  between operations  1.47 us (1%)
    all_to_all x2, blocking collectives, swap(): lax.all_to_all(parts, axes, split_axis=0, concat_axis=0, tiled=True, axis...  32 us
    pallas_call x6, Pallas kernels, whole_call(): pl.pallas_call(kernel, name=name, out_shape=out_shape, in_specs=[smem] *...  21.8 us
    all_to_all x1, starting transfers between devices, on_device(): lax.all_to_all(packed.reshape(bands, CAP_ROWS, LANES), 'lat', split_axis=...  21.6 us
    all_gather x1, blocking collectives, on_device(): normed_all = lax.all_gather(normed, 'lon', axis=0, tiled=True)  13.5 us
    all_gather x1, blocking collectives, on_device(): att_all = lax.all_gather(d_att, 'lon', axis=0, tiled=True)  11.1 us
    all_to_all x1, starting transfers between devices, swap(): lax.all_to_all(parts, axes, split_axis=0, concat_axis=0, tiled=True, axis...  6.2 us
    all_to_all x1, waiting for transfers between devices, swap(): lax.all_to_all(parts, axes, split_axis=0, concat_axis=0, tiled=True, axis...  5.05 us
  transfers between devices with their start and end apart: 2, of which 2 were waited for; matrix products, arithmetic and copies ran while one was open for 4% of the time, Pallas kernels for 3%

profile of v3, /device:TPU:1, one launch (start us, length us, event | category | flops | bytes accessed | tf_op | source)
XLA Modules:
  0.0 119.5 jit_solution(7796194085841338120)
XLA Ops:
  0.6 0.0 copy-start
  1.4 2.1 %pack.1 = bf16[1024,128]{1,0:T(8,128)(2,1)} custom-call(s32[1]{0:T(128)S(6)} %copy.21.count_ref, s32[1,512]{1,0:T(1,128)} %bitcast.27, s32[1,512]{1,0:T(1,128)} %bitcast.28, s32[1,512]{1,0:T(1,128)} %bitcast.29, bf16[64,512]{1,0:T(8,128)(2,1)} %bitcast.26), custom_call_target="tpu_custom_call" | custom-call | tf_op jit(solution)/shard_map/pack/pallas_call | solution.py:514
  3.5 0.0 copy-start.1
  3.5 0.0 copy-start.2
  3.5 21.6 %all-to-all-start = ((bf16[128,8,128]{2,1,0:T(8,128)(2,1)}), bf16[128,8,128]{2,1,0:T(8,128)(2,1)S(1)}, u32[]{:S(2)}, u32[]{:S(2)}) async-start(bf16[128,8,128]{2,1,0:T(8,128)(2,1)} %bitcast.4), calls=%async_computation | async-start | bytes 524288 | tf_op jit(solution)/shard_map/all_to_all | solution.py:716
  25.1 0.7 reshape.50
  25.7 0.7 reshape.51
  26.4 0.7 stack.19
  27.1 0.1 pad.3.clone
  27.2 0.7 maximum_maximum_fusion.lines_ref
  27.9 0.0 copy-done
  27.9 1.3 %convolution_convert_fusion = bf16[128,640]{1,0:T(8,128)(2,1)S(1)} fusion(bf16[640,640]{1,0:T(8,128)(2,1)S(1)} %copy-done, bf16[1,128,640]{2,1,0:T(8,128)(2,1)} %param.19), kind=kOutput, calls=%fused_computation | convolution fusion | flops 104939520 | bytes 1146880 | tf_op jit(solution)/shard_map/dot_general | solution.py:40
  29.2 11.1 %all_gather.7.att_ref = bf16[512,640]{1,0:T(8,128)(2,1)S(1)} all-gather(bf16[128,640]{1,0:T(8,128)(2,1)S(1)} %convolution_convert_fusion), channel_id=1, replica_groups=mesh['lat'=128,'lon'=4] {'lon'}, dimensions={0}, use_global_device_ids=true | all-gather | bytes 819200 | tf_op jit(solution)/shard_map/all_gather | solution.py:721
  40.3 0.0 copy-done.1
  40.3 0.0 copy-done.2
  40.3 1.0 convolution_convert_fusion.1.query_ref
  41.3 0.8 all-to-all-done
  42.1 4.9 %cross_forward.1 = (bf16[128,640]{1,0:T(8,128)(2,1)S(1)}, bf16[128,640]{1,0:T(8,128)(2,1)S(1)}, bf16[1024,640]{1,0:T(8,128)(2,1)}, bf16[1024,640]{1,0:T(8,128)(2...) custom-call(bf16[1024,128]{1,0:T(8,128)(2,1)S(1)} %bitcast.18, ...), custom_call_target="tpu_custom_call" | custom-call | tf_op jit(solution)/shard_map/cross_forward/pallas_call | solution.py:514
  47.1 13.5 %all_gather.6.normed_ref = bf16[512,640]{1,0:T(8,128)(2,1)S(1)} all-gather(bf16[128,640]{1,0:T(8,128)(2,1)S(1)} %get-tuple-element.23), channel_id=1, replica_groups=mesh['lat'=128,'lon'=4] {'lon'}, dimensions={0}, use_global_device_ids=true | all-gather | bytes 819200 | tf_op jit(solution)/shard_map/all_gather | solution.py:735
  60.6 7.9 %zonal.1.dres_ref = bf16[128,640]{1,0:T(8,128)(2,1)S(1)} custom-call(s32[1]{0:T(128)} %bitcast.6.me_ref, bf16[512,640]{1,0:T(8,128)(2,1)S(1)} %all_gather.6.normed_ref, bf16[512,640]{1,0:T(8,128)(2,1)S(1)} %all_gather.7.att_ref, bf16[640,640]{1,0:T(8,128)(2,1)S(1)} %get-tuple-element.24.zq_ref, bf16[640,640]{1,0:T(8,128)(2,1)S(1)} %get-tuple-element.25.zk_ref, ...), custom_call_target="tpu_custom_call" | custom-call | tf_op jit(solution)/shard_map/zonal/pallas_call | solution.py:514
  68.5 3.0 %cross_backward.1 = (bf16[768,128]{1,0:T(8,128)(2,1)S(1)}, bf16[1024,128]{1,0:T(8,128)(2,1)S(1)}, f32[128,128]{1,0:T(8,128)S(1)}) custom-call(bf16[1024,128]{1,0:T(8,128)(2,1)S(1)} %bitcast.19, bf16[128,640]{1,0:T(8,128)(2,1)S(1)} %zonal.1.dres_ref, f32[8,640]{1,0:T(8,128)S(1)} %get-tuple-element.29.lines_ref, ...), custom_call_target="tpu_custom_call" | custom-call | tf_op jit(solution)/shard_map/cross_backward/pallas_call | solution.py:514
  71.5 14.6 %all_to_all.20 = bf16[32,24,128]{2,1,0:T(8,128)(2,1)S(1)} all-to-all(bf16[32,24,128]{2,1,0:T(8,128)(2,1)S(1)} %bitcast.22), channel_id=1, replica_groups={{0,1,2,3,4,5,6,7,8,9,10,11,12,13,14,15,16,17,18,19,20,21,22,23,24,25,26..., dimensions={0} | all-to-all | bytes 393216 | tf_op jit(solution)/shard_map/all_to_all | solution.py:672
  86.1 17.5 %all_to_all.21 = bf16[16,24,128]{2,1,0:T(8,128)(2,1)S(1)} all-to-all(bf16[16,24,128]{2,1,0:T(8,128)(2,1)S(1)} %broadcast_in_dim.10), channel_id=1, replica_groups={{0,32,64,96,128,160,192,224,256,288,320,352,384,416,448,480},{4,36,68,1..., dimensions={0} | all-to-all | bytes 196608 | tf_op jit(solution)/shard_map/all_to_all | solution.py:672
  103.6 0.7 broadcast_in_dim.11
  104.4 6.2 %all-to-all-start.3 = ((bf16[32,24,128]{2,1,0:T(8,128)(2,1)}), bf16[32,24,128]{2,1,0:T(8,128)(2,1)S(1)}, u32[]{:S(2)}, u32[]{:S(2)}) async-start(bf16[32,24,128]{2,1,0:T(8,128)(2,1)} %broadcast_in_dim.11), calls=%async_computation.3 | async-start | bytes 393216 | tf_op jit(solution)/shard_map/all_to_all | solution.py:672
  110.6 3.1 %token_gradient.1 = bf16[128,640]{1,0:T(8,128)(2,1)} custom-call(bf16[1024,128]{1,0:T(8,128)(2,1)S(1)} %bitcast.20, bf16[128,640]{1,0:T(8,128)(2,1)S(1)} %zonal.1.dres_ref, f32[8,640]{1,0:T(8,128)S(1)} %get-tuple-element.29.lines_ref, bf16[1024,128]{1,0:T(8,128)(2,1)S(1)} %get-tuple-element.37.draw_ref, f32[128,128]{1,0:T(8,128)S(1)} %get-tuple-element.38.nraw_ref, ...), custom_call_target="tpu_custom_call" | custom-call | tf_op jit(solution)/shard_map/token_gradient/pallas_call | solution.py:514
  113.7 5.1 %all-to-all-done.3 = bf16[32,24,128]{2,1,0:T(8,128)(2,1)S(1)} async-done(((bf16[32,24,128]{2,1,0:T(8,128)(2,1)}), bf16[32,24,128]{2,1,0:T(8,128)(2,1)S(1)}, u32[]{:S(2)}, u32[]{:S(2)}) %all-to-all-start.3) | async-done | bytes 196640 | tf_op jit(solution)/shard_map/all_to_all | solution.py:672
  118.8 0.7 unpack.1
  (4 shorter events, 0.1 us)
Async XLA Ops:
  0.6 27.2 %copy-start = (bf16[640,640]{1,0:T(8,128)(2,1)S(1)}, bf16[640,640]{1,0:T(8,128)(2,1)}, u32[]{:S(2)}) copy-start(bf16[640,640]{1,0:T(8,128)(2,1)} %param.35) | copy-start | bytes 2457604
  3.5 36.9 %copy-start.1 = (bf16[640,640]{1,0:T(8,128)(2,1)S(1)}, bf16[640,640]{1,0:T(8,128)(2,1)}, u32[]{:S(2)}) copy-start(bf16[640,640]{1,0:T(8,128)(2,1)} %wq_ref.1) | copy-start | bytes 2457604
  3.5 36.9 %copy-start.2 = (bf16[1,128,640]{2,1,0:T(8,128)(2,1)S(1)}, bf16[1,128,640]{2,1,0:T(8,128)(2,1)}, u32[]{:S(2)}) copy-start(bf16[1,128,640]{2,1,0:T(8,128)(2,1)} %param.18) | copy-start | bytes 491524
  3.5 38.7 %all-to-all-start = ((bf16[128,8,128]{2,1,0:T(8,128)(2,1)}), bf16[128,8,128]{2,1,0:T(8,128)(2,1)S(1)}, u32[]{:S(2)}, u32[]{:S(2)}) async-start(bf16[128,8,128]{2,1,0:T(8,128)(2,1)} %bitcast.4), calls=%async_computation | async-start | bytes 524288 | tf_op jit(solution)/shard_map/all_to_all | solution.py:716
  104.4 14.4 %all-to-all-start.3 = ((bf16[32,24,128]{2,1,0:T(8,128)(2,1)}), bf16[32,24,128]{2,1,0:T(8,128)(2,1)S(1)}, u32[]{:S(2)}, u32[]{:S(2)}) async-start(bf16[32,24,128]{2,1,0:T(8,128)(2,1)} %broadcast_in_dim.11), calls=%async_computation.3 | async-start | bytes 393216 | tf_op jit(solution)/shard_map/all_to_all | solution.py:672

commit v4 on v3

--- a/solution.py
+++ b/solution.py
@@ -146,6 +146,27 @@
         leaving[-1].start()
     for move in leaving:
         move.wait()
+
+
+def ready_kernel(
+    tok_ref,
+    cot_ref,
+    wq_ref,
+    zo_ref,
+    nk_ref,
+    nv_ref,
+    gain_ref,
+    att_ref,
+    query_ref,
+    lines_ref,
+):
+    att_ref[...] = dot_nt(cot_ref[...], zo_ref[...]).astype(bf16)
+    query_ref[...] = dot_nn(tok_ref[...], wq_ref[...]).astype(bf16)
+    lines_ref[...] = jnp.zeros(lines_ref.shape, f32)
+    for row, ref in enumerate((nk_ref, nv_ref, gain_ref)):
+        for k in range(ref.shape[0]):
+            cols = slice(k * LANES, (k + 1) * LANES)
+            lines_ref[row : row + 1, cols] = ref[k : k + 1, :].astype(f32)
 
 
 def cross_kernel(
@@ -283,13 +304,13 @@
 def zonal_kernel(
     me_ref,
     normed_ref,
-    att_ref,
     zq_ref,
     zk_ref,
     zv_ref,
     resid_ref,
     cot_ref,
     lines_ref,
+    att_ref,
     dres_ref,
     zq_s,
     zk_s,
@@ -312,9 +333,6 @@
     for k in range(sectors):
         src = pl.multiple_of(lax.rem(me + k, sectors) * own, own)
         norm_s[k * own : (k + 1) * own, :] = normed_ref[pl.ds(src, own), :]
-        part = att_ref[pl.ds(src, own), :]
-        for p in range(pairs):
-            att_s[p, k * own : (k + 1) * own, :] = part[:, p * LANES : (p + 1) * LANES]
     normed = norm_s[...]
     for ref, out in ((zq_ref, zq_s), (zk_ref, zk_s), (zv_ref, zv_s)):
         proj = dot_nn(normed, ref[...])
@@ -323,6 +341,11 @@
             out[p] = piece.astype(bf16)
             if out is zk_s:
                 zkt_s[p] = piece.astype(bf16).T
+    for k in range(sectors):
+        src = pl.multiple_of(lax.rem(me + k, sectors) * own, own)
+        part = att_ref[pl.ds(src, own), :]
+        for p in range(pairs):
+            att_s[p, k * own : (k + 1) * own, :] = part[:, p * LANES : (p + 1) * LANES]
     lane_head = iota((whole, LANES), 1) // HEAD_DIM
     low_half = iota((own, LANES), 1) < HEAD_DIM
 
@@ -562,6 +585,24 @@
     )[0]
 
 
+def get_ready(tok, cot, w_query, zonal_out, null_key, null_val, gain):
+    toks, width = tok.shape
+    args = (tok, cot, w_query, zonal_out) + tuple(
+        v.reshape(width // LANES, LANES) for v in (null_key, null_val, gain)
+    )
+    return whole_call(
+        ready_kernel,
+        "get_ready",
+        [
+            plain(toks, width, bf16),
+            pltpu.HBM((toks, width), bf16),
+            pltpu.HBM((8, width), f32),
+        ],
+        args,
+        fetched=len(args),
+    )
+
+
 def cross_forward(x, w_key, w_val, table, query, lines, tok, cot, zq, zk, zv):
     slots = x.shape[0]
     toks, width = tok.shape
@@ -602,7 +643,7 @@
         zonal_kernel,
         "zonal",
         shaped(own, width, bf16),
-        (me, normed_all, att_all, zq, zk, zv, resid, cot, lines),
+        (me, normed_all, zq, zk, zv, resid, cot, lines, att_all),
         scalars=1,
         scratch=(
             rows,
@@ -710,14 +751,13 @@
     obs_total = raw_obs.shape[0] * devices
     tok = tokens.reshape(tok_rows, width)
     cot = cotangent.reshape(tok_rows, width)
-    lines = jnp.stack([null_key.astype(f32), null_val.astype(f32), norm_gain])
-    lines = jnp.concatenate([lines, jnp.zeros((5, width), f32)], axis=0)
     packed = pack(obs_count, obs_band, obs_slot, obs_inst, raw_obs, bands)
     received = lax.all_to_all(
         packed.reshape(bands, CAP_ROWS, LANES), "lat", split_axis=0, concat_axis=0, tiled=True
     ).reshape(bands * CAP_ROWS, LANES)
-    query = jnp.dot(tok, w_query, preferred_element_type=f32).astype(bf16)
-    d_att = dot_nt(cot, zonal_out).astype(bf16)
+    d_att, query, lines = get_ready(
+        tok, cot, w_query, zonal_out, null_key, null_val, norm_gain
+    )
     att_all = lax.all_gather(d_att, "lon", axis=0, tiled=True)
     resid, normed, keys, *saved, lines, cot, zq, zk, zv = cross_forward(
         received,

time: 120 us -> 118 us (0.983)
  Pallas kernels: 21.8 us -> 24.6 us
  waiting for transfers between devices: 5.9 us -> 8.49 us
  blocking collectives: 56.7 us -> 54.4 us
  matrix products: 2.26 us -> 0 us
  local copies, waits for them, and re-layouts: 2.9 us -> 0.73 us
    pallas_call x6 -> x7, Pallas kernels: 21.8 us -> 24.6 us  [whole_call(): pl.pallas_call(kernel, name=name, out_shape=out_shape, in_specs=[smem] *...]
    all_to_all x1, waiting for transfers between devices: 0.84 us -> 3.44 us  [on_device(): lax.all_to_all(packed.reshape(bands, CAP_ROWS, LANES), 'lat', split_axis=...]
    dot_general x2 -> x0, matrix products: 2.26 us -> none  [the longest x1 1.28 us: dot_nt(): lax.dot_general(a, b, (((1,), (1,)), ((), ())), preferred_element_type=f32)]
    another operation x3 -> x0, local copies, waits for them, and re-layouts: 2.06 us -> none  [on_device(): lines = jnp.stack([null_key.astype(f32), null_val.astype(f32), norm_gain])]
    all_to_all x2, blocking collectives: 32 us -> 30 us  [swap(): lax.all_to_all(parts, axes, split_axis=0, concat_axis=0, tiled=True, axis...]
  transfers between devices with their start and end apart: 2 -> 2, of which waited for: 2 -> 2; matrix products, arithmetic and copies ran while one was open for 4% -> 0% of each run, Pallas kernels for 3% -> 5%
where the time goes in v4:
time: 118 us; the launch traced here: 117 us
  blocking collectives  54.4 us (46%)
  starting transfers between devices  27.6 us (23%)
  Pallas kernels  24.6 us (21%)
  waiting for transfers between devices  8.49 us (7%)
  between operations  1.35 us (1%)
    all_to_all x2, blocking collectives, swap(): lax.all_to_all(parts, axes, split_axis=0, concat_axis=0, tiled=True, axis...  30 us
    pallas_call x7, Pallas kernels, whole_call(): pl.pallas_call(kernel, name=name, out_shape=out_shape, in_specs=[smem] *...  24.6 us
    all_to_all x1, starting transfers between devices, on_device(): lax.all_to_all(packed.reshape(bands, CAP_ROWS, LANES), 'lat', split_axis=...  21.4 us
    all_gather x1, blocking collectives, on_device(): normed_all = lax.all_gather(normed, 'lon', axis=0, tiled=True)  13.5 us
    all_gather x1, blocking collectives, on_device(): att_all = lax.all_gather(d_att, 'lon', axis=0, tiled=True)  10.9 us
    all_to_all x1, starting transfers between devices, swap(): lax.all_to_all(parts, axes, split_axis=0, concat_axis=0, tiled=True, axis...  6.2 us
    all_to_all x1, waiting for transfers between devices, swap(): lax.all_to_all(parts, axes, split_axis=0, concat_axis=0, tiled=True, axis...  5.05 us
    all_to_all x1, waiting for transfers between devices, on_device(): lax.all_to_all(packed.reshape(bands, CAP_ROWS, LANES), 'lat', split_axis=...  3.44 us
  transfers between devices with their start and end apart: 2, of which 2 were waited for; matrix products, arithmetic and copies ran while one was open for 0% of the time, Pallas kernels for 5%

profile of v4, /device:TPU:1, one launch (start us, length us, event | category | flops | bytes accessed | tf_op | source)
XLA Modules:
  0.0 117.2 jit_solution(7865571296510636930)
XLA Ops:
  1.3 2.1 %pack.1 = bf16[1024,128]{1,0:T(8,128)(2,1)} custom-call(s32[1]{0:T(128)S(6)} %copy.21.count_ref, s32[1,512]{1,0:T(1,128)} %bitcast.27, s32[1,512]{1,0:T(1,128)} %bitcast.28, s32[1,512]{1,0:T(1,128)} %bitcast.29, bf16[64,512]{1,0:T(8,128)(2,1)} %bitcast.25), custom_call_target="tpu_custom_call" | custom-call | tf_op jit(solution)/shard_map/pack/pallas_call | solution.py:537
  3.4 21.4 %all-to-all-start = ((bf16[128,8,128]{2,1,0:T(8,128)(2,1)}), bf16[128,8,128]{2,1,0:T(8,128)(2,1)S(1)}, u32[]{:S(2)}, u32[]{:S(2)}) async-start(bf16[128,8,128]{2,1,0:T(8,128)(2,1)} %bitcast.4), calls=%async_computation | async-start | bytes 524288 | tf_op jit(solution)/shard_map/all_to_all | solution.py:755
  24.8 2.8 %get_ready.1 = (bf16[128,640]{1,0:T(8,128)(2,1)S(1)}, bf16[128,640]{1,0:T(8,128)(2,1)}, f32[8,640]{1,0:T(8,128)}) custom-call(bf16[128,640]{1,0:T(8,128)(2,1)} %bitcast.20, bf16[128,640]{1,0:T(8,128)(2,1)} %bitcast.22, bf16[640,640]{1,0:T(8,128)(2,1)} %wq_ref.3, bf16[640,640]{1,0:T(8,128)(2,1)} %zo_ref.1, bf16[5,128]{1,0:T(8,128)(2,1)} %bitcast.30, ...), custom_call_target="tpu_custom_call" | custom-call | tf_op jit(solution)/shard_map/get_ready/pallas_call | solution.py:537
  27.6 10.9 %all_gather.7.att_ref = bf16[512,640]{1,0:T(8,128)(2,1)S(1)} all-gather(bf16[128,640]{1,0:T(8,128)(2,1)S(1)} %get-tuple-element.35), channel_id=1, replica_groups=mesh['lat'=128,'lon'=4] {'lon'}, dimensions={0}, use_global_device_ids=true | all-gather | bytes 819200 | tf_op jit(solution)/shard_map/all_gather | solution.py:761
  38.5 3.4 %all-to-all-done = bf16[128,8,128]{2,1,0:T(8,128)(2,1)S(1)} async-done(((bf16[128,8,128]{2,1,0:T(8,128)(2,1)}), bf16[128,8,128]{2,1,0:T(8,128)(2,1)S(1)}, u32[]{:S(2)}, u32[]{:S(2)}) %all-to-all-start) | async-done | bytes 262176 | tf_op jit(solution)/shard_map/all_to_all | solution.py:755
  41.9 4.9 %cross_forward.1 = (bf16[128,640]{1,0:T(8,128)(2,1)S(1)}, bf16[128,640]{1,0:T(8,128)(2,1)S(1)}, bf16[1024,640]{1,0:T(8,128)(2,1)}, bf16[1024,640]{1,0:T(8,128)(2...) custom-call(bf16[1024,128]{1,0:T(8,128)(2,1)S(1)} %bitcast.15, ...), custom_call_target="tpu_custom_call" | custom-call | tf_op jit(solution)/shard_map/cross_forward/pallas_call | solution.py:537
  46.8 13.5 %all_gather.6.normed_ref = bf16[512,640]{1,0:T(8,128)(2,1)S(1)} all-gather(bf16[128,640]{1,0:T(8,128)(2,1)S(1)} %get-tuple-element.28), channel_id=1, replica_groups=mesh['lat'=128,'lon'=4] {'lon'}, dimensions={0}, use_global_device_ids=true | all-gather | bytes 819200 | tf_op jit(solution)/shard_map/all_gather | solution.py:775
  60.4 7.9 %zonal.1.dres_ref = bf16[128,640]{1,0:T(8,128)(2,1)S(1)} custom-call(s32[1]{0:T(128)} %bitcast.6.me_ref, bf16[512,640]{1,0:T(8,128)(2,1)S(1)} %all_gather.6.normed_ref, bf16[640,640]{1,0:T(8,128)(2,1)S(1)} %get-tuple-element.29.zq_ref, bf16[640,640]{1,0:T(8,128)(2,1)S(1)} %get-tuple-element.30.zk_ref, bf16[640,640]{1,0:T(8,128)(2,1)S(1)} %get-tuple-element.31.zv_ref, ...), custom_call_target="tpu_custom_call" | custom-call | tf_op jit(solution)/shard_map/zonal/pallas_call | solution.py:537
  68.2 3.0 %cross_backward.1 = (bf16[768,128]{1,0:T(8,128)(2,1)S(1)}, bf16[1024,128]{1,0:T(8,128)(2,1)S(1)}, f32[128,128]{1,0:T(8,128)S(1)}) custom-call(bf16[1024,128]{1,0:T(8,128)(2,1)S(1)} %bitcast.16, bf16[128,640]{1,0:T(8,128)(2,1)S(1)} %zonal.1.dres_ref, f32[8,640]{1,0:T(8,128)S(1)} %get-tuple-element.34.lines_ref, ...), custom_call_target="tpu_custom_call" | custom-call | tf_op jit(solution)/shard_map/cross_backward/pallas_call | solution.py:537
  71.2 14.5 %all_to_all.20 = bf16[32,24,128]{2,1,0:T(8,128)(2,1)S(1)} all-to-all(bf16[32,24,128]{2,1,0:T(8,128)(2,1)S(1)} %bitcast.19), channel_id=1, replica_groups={{0,1,2,3,4,5,6,7,8,9,10,11,12,13,14,15,16,17,18,19,20,21,22,23,24,25,26..., dimensions={0} | all-to-all | bytes 393216 | tf_op jit(solution)/shard_map/all_to_all | solution.py:713
  85.9 15.5 %all_to_all.21 = bf16[16,24,128]{2,1,0:T(8,128)(2,1)S(1)} all-to-all(bf16[16,24,128]{2,1,0:T(8,128)(2,1)S(1)} %broadcast_in_dim.6), channel_id=1, replica_groups={{0,32,64,96,128,160,192,224,256,288,320,352,384,416,448,480},{4,36,68,1..., dimensions={0} | all-to-all | bytes 196608 | tf_op jit(solution)/shard_map/all_to_all | solution.py:713
  101.4 0.7 broadcast_in_dim.7
  102.1 6.2 %all-to-all-start.3 = ((bf16[32,24,128]{2,1,0:T(8,128)(2,1)}), bf16[32,24,128]{2,1,0:T(8,128)(2,1)S(1)}, u32[]{:S(2)}, u32[]{:S(2)}) async-start(bf16[32,24,128]{2,1,0:T(8,128)(2,1)} %broadcast_in_dim.7), calls=%async_computation.3 | async-start | bytes 393216 | tf_op jit(solution)/shard_map/all_to_all | solution.py:713
  108.3 3.1 %token_gradient.1 = bf16[128,640]{1,0:T(8,128)(2,1)} custom-call(bf16[1024,128]{1,0:T(8,128)(2,1)S(1)} %bitcast.17, bf16[128,640]{1,0:T(8,128)(2,1)S(1)} %zonal.1.dres_ref, f32[8,640]{1,0:T(8,128)S(1)} %get-tuple-element.34.lines_ref, bf16[1024,128]{1,0:T(8,128)(2,1)S(1)} %get-tuple-element.43.draw_ref, f32[128,128]{1,0:T(8,128)S(1)} %get-tuple-element.44.nraw_ref, ...), custom_call_target="tpu_custom_call" | custom-call | tf_op jit(solution)/shard_map/token_gradient/pallas_call | solution.py:537
  111.4 5.1 %all-to-all-done.3 = bf16[32,24,128]{2,1,0:T(8,128)(2,1)S(1)} async-done(((bf16[32,24,128]{2,1,0:T(8,128)(2,1)}), bf16[32,24,128]{2,1,0:T(8,128)(2,1)S(1)}, u32[]{:S(2)}, u32[]{:S(2)}) %all-to-all-start.3) | async-done | bytes 196640 | tf_op jit(solution)/shard_map/all_to_all | solution.py:713
  116.5 0.7 unpack.1
  (3 shorter events, 0.1 us)
Async XLA Ops:
  3.4 38.5 %all-to-all-start = ((bf16[128,8,128]{2,1,0:T(8,128)(2,1)}), bf16[128,8,128]{2,1,0:T(8,128)(2,1)S(1)}, u32[]{:S(2)}, u32[]{:S(2)}) async-start(bf16[128,8,128]{2,1,0:T(8,128)(2,1)} %bitcast.4), calls=%async_computation | async-start | bytes 524288 | tf_op jit(solution)/shard_map/all_to_all | solution.py:755
  102.1 14.4 %all-to-all-start.3 = ((bf16[32,24,128]{2,1,0:T(8,128)(2,1)}), bf16[32,24,128]{2,1,0:T(8,128)(2,1)S(1)}, u32[]{:S(2)}, u32[]{:S(2)}) async-start(bf16[32,24,128]{2,1,0:T(8,128)(2,1)} %broadcast_in_dim.7), calls=%async_computation.3 | async-start | bytes 393216 | tf_op jit(solution)/shard_map/all_to_all | solution.py:713

commit v5 on v4

--- a/solution.py
+++ b/solution.py
@@ -160,7 +160,7 @@
     query_ref,
     lines_ref,
 ):
-    att_ref[...] = dot_nt(cot_ref[...], zo_ref[...]).astype(bf16)
+    att_ref[...] = dot_nt(cot_ref[...], zo_ref[...]).astype(bf16).astype(f32)
     query_ref[...] = dot_nn(tok_ref[...], wq_ref[...]).astype(bf16)
     lines_ref[...] = jnp.zeros(lines_ref.shape, f32)
     for row, ref in enumerate((nk_ref, nv_ref, gain_ref)):
@@ -181,6 +181,7 @@
     zq_ref,
     zk_ref,
     zv_ref,
+    att_ref,
     resid_ref,
     normed_ref,
     key_ref,
@@ -196,6 +197,7 @@
     zq_out,
     zk_out,
     zv_out,
+    att_out,
     both_s,
     query_s,
     tok_s,
@@ -225,6 +227,7 @@
                 (zk_ref, zk_out),
                 (zv_ref, zv_out),
                 (cot_ref, cot_out),
+                (att_ref, att_out),
             )
         )
     ]
@@ -343,7 +346,7 @@
                 zkt_s[p] = piece.astype(bf16).T
     for k in range(sectors):
         src = pl.multiple_of(lax.rem(me + k, sectors) * own, own)
-        part = att_ref[pl.ds(src, own), :]
+        part = att_ref[pl.ds(src, own), :].astype(bf16)
         for p in range(pairs):
             att_s[p, k * own : (k + 1) * own, :] = part[:, p * LANES : (p + 1) * LANES]
     lane_head = iota((whole, LANES), 1) // HEAD_DIM
@@ -594,7 +597,7 @@
         ready_kernel,
         "get_ready",
         [
-            plain(toks, width, bf16),
+            pltpu.HBM((toks, width), f32),
             pltpu.HBM((toks, width), bf16),
             pltpu.HBM((8, width), f32),
         ],
@@ -603,7 +606,7 @@
     )
 
 
-def cross_forward(x, w_key, w_val, table, query, lines, tok, cot, zq, zk, zv):
+def cross_forward(x, w_key, w_val, table, query, lines, tok, cot, zq, zk, zv, att):
     slots = x.shape[0]
     toks, width = tok.shape
     big = shaped(slots, width, bf16)
@@ -611,12 +614,13 @@
     null = shaped(toks, LANES, f32)
     row = shaped(toks, width, bf16)
     square = shaped(*zq.shape, bf16)
-    far = (w_key, w_val, table, query, lines, tok, cot, zq, zk, zv)
+    far = (w_key, w_val, table, query, lines, tok, cot, zq, zk, zv, att)
     return whole_call(
         cross_kernel,
         "cross_forward",
         [row, row, pltpu.HBM((slots, width), bf16), big, big, big, small, small, null, null]
-        + [shaped(*lines.shape, f32), row, square, square, square],
+        + [shaped(*lines.shape, f32), row, square, square, square]
+        + [shaped(*att.shape, f32)],
         (x,) + far,
         far=len(far),
         away=(2,),
@@ -759,7 +763,7 @@
         tok, cot, w_query, zonal_out, null_key, null_val, norm_gain
     )
     att_all = lax.all_gather(d_att, "lon", axis=0, tiled=True)
-    resid, normed, keys, *saved, lines, cot, zq, zk, zv = cross_forward(
+    resid, normed, keys, *saved, lines, cot, zq, zk, zv, att_all = cross_forward(
         received,
         w_key_obs,
         w_val_obs,
@@ -771,6 +775,7 @@
         zonal_query,
         zonal_key,
         zonal_value,
+        att_all,
     )
     normed_all = lax.all_gather(normed, "lon", axis=0, tiled=True)
     me = lax.axis_index("lon").astype(i32).reshape(1)

time: 118 us -> 134 us (1.14)
  waiting for transfers between devices: 8.49 us -> 22.1 us
  between operations: 1.35 us -> 14.8 us
  blocking collectives: 54.4 us -> 43.2 us
    all_to_all x1, waiting for transfers between devices: 3.44 us -> 17.1 us  [on_device(): lax.all_to_all(packed.reshape(bands, CAP_ROWS, LANES), 'lat', split_axis=...]
    all_gather x1 -> x0, blocking collectives: 10.9 us -> none  [on_device(): att_all = lax.all_gather(d_att, 'lon', axis=0, tiled=True)]
  transfers between devices with their start and end apart: 2 -> 3, of which waited for: 2 -> 2; matrix products, arithmetic and copies ran while one was open for 0% -> 0% of each run, Pallas kernels for 5% -> 4%
where the time goes in v5:
time: 134 us; the launch traced here: 133 us
  blocking collectives  43.2 us (32%)
  starting transfers between devices  27.7 us (21%)
  Pallas kernels  24.7 us (18%)
  waiting for transfers between devices  22.1 us (16%)
  between operations  14.8 us (11%)
    all_to_all x2, blocking collectives, swap(): lax.all_to_all(parts, axes, split_axis=0, concat_axis=0, tiled=True, axis...  29.7 us
    pallas_call x7, Pallas kernels, whole_call(): pl.pallas_call(kernel, name=name, out_shape=out_shape, in_specs=[smem] *...  24.7 us
    all_to_all x1, starting transfers between devices, on_device(): lax.all_to_all(packed.reshape(bands, CAP_ROWS, LANES), 'lat', split_axis=...  21.4 us
    all_to_all x1, waiting for transfers between devices, on_device(): lax.all_to_all(packed.reshape(bands, CAP_ROWS, LANES), 'lat', split_axis=...  17.1 us
    all_gather x1, blocking collectives, on_device(): normed_all = lax.all_gather(normed, 'lon', axis=0, tiled=True)  13.5 us
    all_to_all x1, starting transfers between devices, swap(): lax.all_to_all(parts, axes, split_axis=0, concat_axis=0, tiled=True, axis...  6.2 us
    all_to_all x1, waiting for transfers between devices, swap(): lax.all_to_all(parts, axes, split_axis=0, concat_axis=0, tiled=True, axis...  5.05 us
  transfers between devices with their start and end apart: 3, of which 2 were waited for; matrix products, arithmetic and copies ran while one was open for 0% of the time, Pallas kernels for 4%

profile of v5, /device:TPU:1, one launch (start us, length us, event | category | flops | bytes accessed | tf_op | source)
XLA Modules:
  0.0 133.3 jit_solution(11385139610964385991)
XLA Ops:
  7.2 0.0 all-gather.2.cloned.1.call-start
  7.2 2.8 %get_ready.1 = (f32[128,640]{1,0:T(8,128)}, bf16[128,640]{1,0:T(8,128)(2,1)}, f32[8,640]{1,0:T(8,128)}) custom-call(bf16[128,640]{1,0:T(8,128)(2,1)} %bitcast.20, bf16[128,640]{1,0:T(8,128)(2,1)} %bitcast.22, bf16[640,640]{1,0:T(8,128)(2,1)} %wq_ref.3, bf16[640,640]{1,0:T(8,128)(2,1)} %zo_ref.1, bf16[5,128]{1,0:T(8,128)(2,1)} %bitcast.30, ...), custom_call_target="tpu_custom_call" | custom-call | tf_op jit(solution)/shard_map/get_ready/pallas_call | solution.py:540
  10.0 0.0 all-gather.2.cloned.1.call-update
  10.7 2.1 %pack.1 = bf16[1024,128]{1,0:T(8,128)(2,1)} custom-call(s32[1]{0:T(128)S(6)} %copy.21.count_ref, s32[1,512]{1,0:T(1,128)} %bitcast.27, s32[1,512]{1,0:T(1,128)} %bitcast.28, s32[1,512]{1,0:T(1,128)} %bitcast.29, bf16[64,512]{1,0:T(8,128)(2,1)} %bitcast.25), custom_call_target="tpu_custom_call" | custom-call | tf_op jit(solution)/shard_map/pack/pallas_call | solution.py:540
  12.8 21.4 %all-to-all-start = ((bf16[128,8,128]{2,1,0:T(8,128)(2,1)}), bf16[128,8,128]{2,1,0:T(8,128)(2,1)S(1)}, u32[]{:S(2)}, u32[]{:S(2)}) async-start(bf16[128,8,128]{2,1,0:T(8,128)(2,1)} %bitcast.4), calls=%async_computation | async-start | bytes 524288 | tf_op jit(solution)/shard_map/all_to_all | solution.py:759
  34.2 17.1 %all-to-all-done = bf16[128,8,128]{2,1,0:T(8,128)(2,1)S(1)} async-done(((bf16[128,8,128]{2,1,0:T(8,128)(2,1)}), bf16[128,8,128]{2,1,0:T(8,128)(2,1)S(1)}, u32[]{:S(2)}, u32[]{:S(2)}) %all-to-all-start) | async-done | bytes 262176 | tf_op jit(solution)/shard_map/all_to_all | solution.py:759
  51.3 0.0 all-gather.2.cloned.1.call-done.att_ref
  51.3 5.1 %cross_forward.1 = (bf16[128,640]{1,0:T(8,128)(2,1)S(1)}, bf16[128,640]{1,0:T(8,128)(2,1)S(1)}, bf16[1024,640]{1,0:T(8,128)(2,1)}, bf16[1024,640]{1,0:T(8,128)(2...) custom-call(bf16[1024,128]{1,0:T(8,128)(2,1)S(1)} %bitcast.15, ...), custom_call_target="tpu_custom_call" | custom-call | tf_op jit(solution)/shard_map/cross_forward/pallas_call | solution.py:540
  56.4 13.5 %all_gather.7.normed_ref = bf16[512,640]{1,0:T(8,128)(2,1)S(1)} all-gather(bf16[128,640]{1,0:T(8,128)(2,1)S(1)} %get-tuple-element.30), channel_id=1, replica_groups=mesh['lat'=128,'lon'=4] {'lon'}, dimensions={0}, use_global_device_ids=true | all-gather | bytes 819200 | tf_op jit(solution)/shard_map/all_gather | solution.py:780
  69.9 7.9 %zonal.1.dres_ref = bf16[128,640]{1,0:T(8,128)(2,1)S(1)} custom-call(s32[1]{0:T(128)} %bitcast.6.me_ref, bf16[512,640]{1,0:T(8,128)(2,1)S(1)} %all_gather.7.normed_ref, bf16[640,640]{1,0:T(8,128)(2,1)S(1)} %get-tuple-element.31.zq_ref, bf16[640,640]{1,0:T(8,128)(2,1)S(1)} %get-tuple-element.32.zk_ref, bf16[640,640]{1,0:T(8,128)(2,1)S(1)} %get-tuple-element.33.zv_ref, ...), custom_call_target="tpu_custom_call" | custom-call | tf_op jit(solution)/shard_map/zonal/pallas_call | solution.py:540
  77.8 3.0 %cross_backward.1 = (bf16[768,128]{1,0:T(8,128)(2,1)S(1)}, bf16[1024,128]{1,0:T(8,128)(2,1)S(1)}, f32[128,128]{1,0:T(8,128)S(1)}) custom-call(bf16[1024,128]{1,0:T(8,128)(2,1)S(1)} %bitcast.16, bf16[128,640]{1,0:T(8,128)(2,1)S(1)} %zonal.1.dres_ref, f32[8,640]{1,0:T(8,128)S(1)} %get-tuple-element.36.lines_ref, ...), custom_call_target="tpu_custom_call" | custom-call | tf_op jit(solution)/shard_map/cross_backward/pallas_call | solution.py:540
  80.8 14.5 %all_to_all.20 = bf16[32,24,128]{2,1,0:T(8,128)(2,1)S(1)} all-to-all(bf16[32,24,128]{2,1,0:T(8,128)(2,1)S(1)} %bitcast.19), channel_id=1, replica_groups={{0,1,2,3,4,5,6,7,8,9,10,11,12,13,14,15,16,17,18,19,20,21,22,23,24,25,26..., dimensions={0} | all-to-all | bytes 393216 | tf_op jit(solution)/shard_map/all_to_all | solution.py:717
  95.4 15.2 %all_to_all.21 = bf16[16,24,128]{2,1,0:T(8,128)(2,1)S(1)} all-to-all(bf16[16,24,128]{2,1,0:T(8,128)(2,1)S(1)} %broadcast_in_dim.6), channel_id=1, replica_groups={{0,32,64,96,128,160,192,224,256,288,320,352,384,416,448,480},{4,36,68,1..., dimensions={0} | all-to-all | bytes 196608 | tf_op jit(solution)/shard_map/all_to_all | solution.py:717
  110.6 0.7 broadcast_in_dim.7
  111.3 6.2 %all-to-all-start.3 = ((bf16[32,24,128]{2,1,0:T(8,128)(2,1)}), bf16[32,24,128]{2,1,0:T(8,128)(2,1)S(1)}, u32[]{:S(2)}, u32[]{:S(2)}) async-start(bf16[32,24,128]{2,1,0:T(8,128)(2,1)} %broadcast_in_dim.7), calls=%async_computation.3 | async-start | bytes 393216 | tf_op jit(solution)/shard_map/all_to_all | solution.py:717
  117.5 3.1 %token_gradient.1 = bf16[128,640]{1,0:T(8,128)(2,1)} custom-call(bf16[1024,128]{1,0:T(8,128)(2,1)S(1)} %bitcast.17, bf16[128,640]{1,0:T(8,128)(2,1)S(1)} %zonal.1.dres_ref, f32[8,640]{1,0:T(8,128)S(1)} %get-tuple-element.36.lines_ref, bf16[1024,128]{1,0:T(8,128)(2,1)S(1)} %get-tuple-element.45.draw_ref, f32[128,128]{1,0:T(8,128)S(1)} %get-tuple-element.46.nraw_ref, ...), custom_call_target="tpu_custom_call" | custom-call | tf_op jit(solution)/shard_map/token_gradient/pallas_call | solution.py:540
  120.6 5.0 %all-to-all-done.3 = bf16[32,24,128]{2,1,0:T(8,128)(2,1)S(1)} async-done(((bf16[32,24,128]{2,1,0:T(8,128)(2,1)}), bf16[32,24,128]{2,1,0:T(8,128)(2,1)S(1)}, u32[]{:S(2)}, u32[]{:S(2)}) %all-to-all-start.3) | async-done | bytes 196640 | tf_op jit(solution)/shard_map/all_to_all | solution.py:717
  125.7 0.7 unpack.1
  (3 shorter events, 0.1 us)
Async XLA Ops:
  7.2 44.1 %all-gather.2.cloned.1.call-start = ((), (), s32[]{:S(2)}) async-start(), calls=%async_computation.4 | async-start | bytes 1638400 | tf_op jit(solution)/shard_map/all_gather | solution.py:765
  12.8 38.5 %all-to-all-start = ((bf16[128,8,128]{2,1,0:T(8,128)(2,1)}), bf16[128,8,128]{2,1,0:T(8,128)(2,1)S(1)}, u32[]{:S(2)}, u32[]{:S(2)}) async-start(bf16[128,8,128]{2,1,0:T(8,128)(2,1)} %bitcast.4), calls=%async_computation | async-start | bytes 524288 | tf_op jit(solution)/shard_map/all_to_all | solution.py:759
  111.3 14.4 %all-to-all-start.3 = ((bf16[32,24,128]{2,1,0:T(8,128)(2,1)}), bf16[32,24,128]{2,1,0:T(8,128)(2,1)S(1)}, u32[]{:S(2)}, u32[]{:S(2)}) async-start(bf16[32,24,128]{2,1,0:T(8,128)(2,1)} %broadcast_in_dim.7), calls=%async_computation.3 | async-start | bytes 393216 | tf_op jit(solution)/shard_map/all_to_all | solution.py:717
Sparse Core Ops, SparseCore 0:
  10.1 37.0 all-gather.1

commit v6 on v4

--- a/solution.py
+++ b/solution.py
@@ -191,6 +191,8 @@
     prob_ref,
     ntanh_ref,
     nprob_ref,
+    hot_s,
+    wide_ref,
     lines_out,
     cot_out,
     zq_out,
@@ -200,7 +202,6 @@
     query_s,
     tok_s,
     keys_s,
-    hot_s,
     inst_s,
     weight_s,
     sems,
@@ -290,6 +291,7 @@
         prob = weight_s[span, :] * fine_nn(doubled(hot), share)
         prob_ref[span, :] = prob
         spread = dot_nn(prob.astype(bf16), head_spread).astype(bf16)
+        wide_ref[span, :] = spread
         gathered = gathered + dot_tn(hot, spread * val_ref[span, :])
     resid = (tok_s[...].astype(f32) + gathered).astype(bf16)
     resid_ref[...] = resid
@@ -419,12 +421,13 @@
     prob_ref,
     ntanh_ref,
     nprob_ref,
+    hot_s,
+    wide_ref,
     grad_ref,
     draw_ref,
     nraw_ref,
     ds_s,
     dp_s,
-    hot_s,
 ):
     slots = x_ref.shape[0]
     toks, width = dres_ref.shape
@@ -437,8 +440,7 @@
     inner = null_prob * null_dp
     for start in range(0, slots, ROW_BLOCK):
         span = pl.ds(start, ROW_BLOCK)
-        hot = token_hot(x_ref[span, :])
-        hot_s[span, :] = hot
+        hot = hot_s[span, :]
         d_slot = dot_nn(hot, d_resid).astype(bf16)
         ds_s[span, :] = d_slot
         dp = dot_nn(d_slot * val_ref[span, :], head_sum)
@@ -458,9 +460,8 @@
         ).astype(bf16)
         draw_ref[span, :] = d_raw
         d_raw_wide = dot_nn(d_raw, head_spread).astype(bf16)
-        prob_wide = dot_nn(prob.astype(bf16), head_spread).astype(bf16)
         d_keys = d_raw_wide * qs_ref[span, :]
-        d_pre = (prob_wide * ds_s[span, :]) * slope_ref[span, :]
+        d_pre = (wide_ref[span, :] * ds_s[span, :]) * slope_ref[span, :]
         grads = grads + dot_tn(x_ref[span, :], jnp.concatenate([d_keys, d_pre], axis=1))
     blocks = 2 * width // LANES
     for b in range(blocks):
@@ -472,7 +473,7 @@
 
 
 def token_kernel(
-    x_ref,
+    hot_ref,
     dres_ref,
     lines_ref,
     draw_ref,
@@ -484,7 +485,7 @@
     wq_s,
     sems,
 ):
-    slots = x_ref.shape[0]
+    slots = hot_ref.shape[0]
     keys_move = pltpu.make_async_copy(key_ref, keys_s, sems.at[0])
     wq_move = pltpu.make_async_copy(wq_ref, wq_s, sems.at[1])
     keys_move.start()
@@ -495,7 +496,7 @@
     for start in range(0, slots, ROW_BLOCK):
         span = pl.ds(start, ROW_BLOCK)
         d_raw_wide = dot_nn(draw_ref[span, :], head_spread).astype(bf16)
-        hot = token_hot(x_ref[span, :])
+        hot = hot_ref[span, :]
         d_query = d_query + dot_tn(hot, d_raw_wide * keys_s[span, :])
     wq_move.wait()
     d_tok = dres_ref[...].astype(f32) + dot_nt(d_query.astype(bf16), wq_s[...])
@@ -616,6 +617,7 @@
         cross_kernel,
         "cross_forward",
         [row, row, pltpu.HBM((slots, width), bf16), big, big, big, small, small, null, null]
+        + [shaped(slots, LANES, bf16), big]
         + [shaped(*lines.shape, f32), row, square, square, square],
         (x,) + far,
         far=len(far),
@@ -625,7 +627,6 @@
             pltpu.VMEM((toks, width), bf16),
             pltpu.VMEM((toks, width), bf16),
             pltpu.VMEM((slots, width), bf16),
-            pltpu.VMEM((slots, LANES), bf16),
             pltpu.VMEM((slots, LANES), bf16),
             pltpu.VMEM((slots, LANES), f32),
             pltpu.SemaphoreType.DMA((len(far),)),
@@ -662,7 +663,7 @@
     )
 
 
-def cross_backward(x, d_resid, lines, saved):
+def cross_backward(x, d_resid, lines, saved, hot, wide):
     slots = x.shape[0]
     toks, width = d_resid.shape
     return whole_call(
@@ -673,21 +674,20 @@
             shaped(slots, LANES, bf16),
             shaped(toks, LANES, f32),
         ],
-        (x, d_resid, lines) + tuple(saved),
+        (x, d_resid, lines) + tuple(saved) + (hot, wide),
         scratch=(
             pltpu.VMEM((slots, width), bf16),
             pltpu.VMEM((slots, LANES), f32),
-            pltpu.VMEM((slots, LANES), bf16),
         ),
     )
 
 
-def token_gradient(x, d_resid, lines, keys, d_raw, null_raw, w_query):
+def token_gradient(hot, d_resid, lines, keys, d_raw, null_raw, w_query):
     return whole_call(
         token_kernel,
         "token_gradient",
         plain(*d_resid.shape, bf16),
-        (x, d_resid, lines, d_raw, null_raw, keys, w_query),
+        (hot, d_resid, lines, d_raw, null_raw, keys, w_query),
         far=2,
         scratch=(
             pltpu.VMEM(keys.shape, bf16),
@@ -759,7 +759,7 @@
         tok, cot, w_query, zonal_out, null_key, null_val, norm_gain
     )
     att_all = lax.all_gather(d_att, "lon", axis=0, tiled=True)
-    resid, normed, keys, *saved, lines, cot, zq, zk, zv = cross_forward(
+    resid, normed, keys, *saved, hot, wide, lines, cot, zq, zk, zv = cross_forward(
         received,
         w_key_obs,
         w_val_obs,
@@ -775,8 +775,8 @@
     normed_all = lax.all_gather(normed, "lon", axis=0, tiled=True)
     me = lax.axis_index("lon").astype(i32).reshape(1)
     d_resid = zonal(me, normed_all, att_all, zq, zk, zv, resid, cot, lines)
-    grads, d_raw, null_raw = cross_backward(received, d_resid, lines, saved)
-    d_tok = token_gradient(received, d_resid, lines, keys, d_raw, null_raw, w_query)
+    grads, d_raw, null_raw = cross_backward(received, d_resid, lines, saved, hot, wide)
+    d_tok = token_gradient(hot, d_resid, lines, keys, d_raw, null_raw, w_query)
     key_grad, value_grad = unpack(sum_everywhere(grads), width, 1.0 / math.sqrt(obs_total))
     return d_tok.reshape(1, tok_rows, width), key_grad, value_grad
 

time: 118 us -> 117 us (level)
  no operation moved by 1% of the time
where the time goes in v6:
time: 117 us
  blocking collectives  54.4 us (46%)
  starting transfers between devices  27.6 us (24%)
  Pallas kernels  24.3 us (21%)
  waiting for transfers between devices  8.49 us (7%)
  between operations  1.35 us (1%)
    all_to_all x2, blocking collectives, swap(): lax.all_to_all(parts, axes, split_axis=0, concat_axis=0, tiled=True, axis...  30 us
    pallas_call x7, Pallas kernels, whole_call(): pl.pallas_call(kernel, name=name, out_shape=out_shape, in_specs=[smem] *...  24.3 us
    all_to_all x1, starting transfers between devices, on_device(): lax.all_to_all(packed.reshape(bands, CAP_ROWS, LANES), 'lat', split_axis=...  21.4 us
    all_gather x1, blocking collectives, on_device(): normed_all = lax.all_gather(normed, 'lon', axis=0, tiled=True)  13.5 us
    all_gather x1, blocking collectives, on_device(): att_all = lax.all_gather(d_att, 'lon', axis=0, tiled=True)  10.9 us
    all_to_all x1, starting transfers between devices, swap(): lax.all_to_all(parts, axes, split_axis=0, concat_axis=0, tiled=True, axis...  6.2 us
    all_to_all x1, waiting for transfers between devices, swap(): lax.all_to_all(parts, axes, split_axis=0, concat_axis=0, tiled=True, axis...  5.06 us
    all_to_all x1, waiting for transfers between devices, on_device(): lax.all_to_all(packed.reshape(bands, CAP_ROWS, LANES), 'lat', split_axis=...  3.44 us
  transfers between devices with their start and end apart: 2, of which 2 were waited for; matrix products, arithmetic and copies ran while one was open for 0% of the time, Pallas kernels for 5%

profile of v6, /device:TPU:1, one launch (start us, length us, event | category | flops | bytes accessed | tf_op | source)
XLA Modules:
  0.0 116.9 jit_solution(11544517744257317156)
XLA Ops:
  1.3 2.1 %pack.1 = bf16[1024,128]{1,0:T(8,128)(2,1)} custom-call(s32[1]{0:T(128)S(6)} %copy.21.count_ref, s32[1,512]{1,0:T(1,128)} %bitcast.26, s32[1,512]{1,0:T(1,128)} %bitcast.27, s32[1,512]{1,0:T(1,128)} %bitcast.28, bf16[64,512]{1,0:T(8,128)(2,1)} %bitcast.24), custom_call_target="tpu_custom_call" | custom-call | tf_op jit(solution)/shard_map/pack/pallas_call | solution.py:538
  3.4 21.4 %all-to-all-start = ((bf16[128,8,128]{2,1,0:T(8,128)(2,1)}), bf16[128,8,128]{2,1,0:T(8,128)(2,1)S(1)}, u32[]{:S(2)}, u32[]{:S(2)}) async-start(bf16[128,8,128]{2,1,0:T(8,128)(2,1)} %bitcast.4), calls=%async_computation | async-start | bytes 524288 | tf_op jit(solution)/shard_map/all_to_all | solution.py:755
  24.8 2.8 %get_ready.1 = (bf16[128,640]{1,0:T(8,128)(2,1)S(1)}, bf16[128,640]{1,0:T(8,128)(2,1)}, f32[8,640]{1,0:T(8,128)}) custom-call(bf16[128,640]{1,0:T(8,128)(2,1)} %bitcast.19, bf16[128,640]{1,0:T(8,128)(2,1)} %bitcast.21, bf16[640,640]{1,0:T(8,128)(2,1)} %wq_ref.3, bf16[640,640]{1,0:T(8,128)(2,1)} %zo_ref.1, bf16[5,128]{1,0:T(8,128)(2,1)} %bitcast.29, ...), custom_call_target="tpu_custom_call" | custom-call | tf_op jit(solution)/shard_map/get_ready/pallas_call | solution.py:538
  27.6 10.9 %all_gather.7.att_ref = bf16[512,640]{1,0:T(8,128)(2,1)S(1)} all-gather(bf16[128,640]{1,0:T(8,128)(2,1)S(1)} %get-tuple-element.38), channel_id=1, replica_groups=mesh['lat'=128,'lon'=4] {'lon'}, dimensions={0}, use_global_device_ids=true | all-gather | bytes 819200 | tf_op jit(solution)/shard_map/all_gather | solution.py:761
  38.5 3.4 %all-to-all-done = bf16[128,8,128]{2,1,0:T(8,128)(2,1)S(1)} async-done(((bf16[128,8,128]{2,1,0:T(8,128)(2,1)}), bf16[128,8,128]{2,1,0:T(8,128)(2,1)S(1)}, u32[]{:S(2)}, u32[]{:S(2)}) %all-to-all-start) | async-done | bytes 262176 | tf_op jit(solution)/shard_map/all_to_all | solution.py:755
  41.9 5.0 %cross_forward.1 = (bf16[128,640]{1,0:T(8,128)(2,1)S(1)}, bf16[128,640]{1,0:T(8,128)(2,1)S(1)}, bf16[1024,640]{1,0:T(8,128)(2,1)}, bf16[1024,640]{1,0:T(8,128)(2...) custom-call(bf16[1024,128]{1,0:T(8,128)(2,1)S(1)} %bitcast.15, ...), custom_call_target="tpu_custom_call" | custom-call | tf_op jit(solution)/shard_map/cross_forward/pallas_call | solution.py:538
  46.9 13.5 %all_gather.6.normed_ref = bf16[512,640]{1,0:T(8,128)(2,1)S(1)} all-gather(bf16[128,640]{1,0:T(8,128)(2,1)S(1)} %get-tuple-element.31), channel_id=1, replica_groups=mesh['lat'=128,'lon'=4] {'lon'}, dimensions={0}, use_global_device_ids=true | all-gather | bytes 819200 | tf_op jit(solution)/shard_map/all_gather | solution.py:775
  60.4 7.9 %zonal.1.dres_ref = bf16[128,640]{1,0:T(8,128)(2,1)S(1)} custom-call(s32[1]{0:T(128)} %bitcast.11.me_ref, bf16[512,640]{1,0:T(8,128)(2,1)S(1)} %all_gather.6.normed_ref, bf16[640,640]{1,0:T(8,128)(2,1)S(1)} %get-tuple-element.32.zq_ref, bf16[640,640]{1,0:T(8,128)(2,1)S(1)} %get-tuple-element.33.zk_ref, bf16[640,640]{1,0:T(8,128)(2,1)S(1)} %get-tuple-element.34.zv_ref, ...), custom_call_target="tpu_custom_call" | custom-call | tf_op jit(solution)/shard_map/zonal/pallas_call | solution.py:538
  68.2 2.7 %cross_backward.1 = (bf16[768,128]{1,0:T(8,128)(2,1)S(1)}, bf16[1024,128]{1,0:T(8,128)(2,1)S(1)}, f32[128,128]{1,0:T(8,128)S(1)}) custom-call(bf16[1024,128]{1,0:T(8,128)(2,1)S(1)} %bitcast.16, bf16[128,640]{1,0:T(8,128)(2,1)S(1)} %zonal.1.dres_ref, f32[8,640]{1,0:T(8,128)S(1)} %get-tuple-element.37.lines_ref, ...), custom_call_target="tpu_custom_call" | custom-call | tf_op jit(solution)/shard_map/cross_backward/pallas_call | solution.py:538
  71.0 14.5 %all_to_all.20 = bf16[32,24,128]{2,1,0:T(8,128)(2,1)S(1)} all-to-all(bf16[32,24,128]{2,1,0:T(8,128)(2,1)S(1)} %bitcast.18), channel_id=1, replica_groups={{0,1,2,3,4,5,6,7,8,9,10,11,12,13,14,15,16,17,18,19,20,21,22,23,24,25,26..., dimensions={0} | all-to-all | bytes 393216 | tf_op jit(solution)/shard_map/all_to_all | solution.py:713
  85.6 15.5 %all_to_all.21 = bf16[16,24,128]{2,1,0:T(8,128)(2,1)S(1)} all-to-all(bf16[16,24,128]{2,1,0:T(8,128)(2,1)S(1)} %broadcast_in_dim.6), channel_id=1, replica_groups={{0,32,64,96,128,160,192,224,256,288,320,352,384,416,448,480},{4,36,68,1..., dimensions={0} | all-to-all | bytes 196608 | tf_op jit(solution)/shard_map/all_to_all | solution.py:713
  101.1 0.7 broadcast_in_dim.7
  101.8 6.2 %all-to-all-start.3 = ((bf16[32,24,128]{2,1,0:T(8,128)(2,1)}), bf16[32,24,128]{2,1,0:T(8,128)(2,1)S(1)}, u32[]{:S(2)}, u32[]{:S(2)}) async-start(bf16[32,24,128]{2,1,0:T(8,128)(2,1)} %broadcast_in_dim.7), calls=%async_computation.3 | async-start | bytes 393216 | tf_op jit(solution)/shard_map/all_to_all | solution.py:713
  108.0 3.1 %token_gradient.1 = bf16[128,640]{1,0:T(8,128)(2,1)} custom-call(bf16[1024,128]{1,0:T(8,128)(2,1)S(1)} %get-tuple-element.30.hot_s.hot_ref, bf16[128,640]{1,0:T(8,128)(2,1)S(1)} %zonal.1.dres_ref, f32[8,640]{1,0:T(8,128)S(1)} %get-tuple-element.37.lines_ref, bf16[1024,128]{1,0:T(8,128)(2,1)S(1)} %get-tuple-element.47.draw_ref, ...), custom_call_target="tpu_custom_call" | custom-call | tf_op jit(solution)/shard_map/token_gradient/pallas_call | solution.py:538
  111.2 5.1 %all-to-all-done.3 = bf16[32,24,128]{2,1,0:T(8,128)(2,1)S(1)} async-done(((bf16[32,24,128]{2,1,0:T(8,128)(2,1)}), bf16[32,24,128]{2,1,0:T(8,128)(2,1)S(1)}, u32[]{:S(2)}, u32[]{:S(2)}) %all-to-all-start.3) | async-done | bytes 196640 | tf_op jit(solution)/shard_map/all_to_all | solution.py:713
  116.2 0.7 unpack.1
  (3 shorter events, 0.1 us)
Async XLA Ops:
  3.4 38.5 %all-to-all-start = ((bf16[128,8,128]{2,1,0:T(8,128)(2,1)}), bf16[128,8,128]{2,1,0:T(8,128)(2,1)S(1)}, u32[]{:S(2)}, u32[]{:S(2)}) async-start(bf16[128,8,128]{2,1,0:T(8,128)(2,1)} %bitcast.4), calls=%async_computation | async-start | bytes 524288 | tf_op jit(solution)/shard_map/all_to_all | solution.py:755
  101.8 14.4 %all-to-all-start.3 = ((bf16[32,24,128]{2,1,0:T(8,128)(2,1)}), bf16[32,24,128]{2,1,0:T(8,128)(2,1)S(1)}, u32[]{:S(2)}, u32[]{:S(2)}) async-start(bf16[32,24,128]{2,1,0:T(8,128)(2,1)} %broadcast_in_dim.7), calls=%async_computation.3 | async-start | bytes 393216 | tf_op jit(solution)/shard_map/all_to_all | solution.py:713
